TPU v7x, 32 devices: a whole 2x2x4 slice. The times are simulated.
32 devices in a mesh: groups: 2 (over x), seq: 16 (over z, y, core).
Axes of the slice: x: 2, y: 2, z: 4, core: 2. Of those that a mesh axis runs over, the one named last changes fastest.
Arguments:
- latents: bfloat16 [2304, 128, 512], P(('groups', 'seq')), parts along dimension 0, may hold values from -6 to 6
- queries: bfloat16 [96, 4, 8192], P(('groups', 'seq')), parts along dimension 0, may hold values from -240 to 240
- new_latents: bfloat16 [96, 4, 512], P(('groups', 'seq')), parts along dimension 0, may hold values from -6 to 6
- up_proj: bfloat16 [2, 256, 1024], P(None, 'seq'), may hold values from -0.375 to 0.375
- lengths: int32 [96], P('groups'), parts along dimension 0, may hold values from 1152 to 3072, as said below
- place: int32 [96], P('groups'), parts along dimension 0, may hold values from 0 to 47, as said below
- block_src: int32 [96, 24], P('groups'), parts along dimension 0, may hold values from 0 to 15, as said below
- block_slot: int32 [96, 24], P('groups'), parts along dimension 0, may hold values from 0 to 71
Outputs:
- attn_out: bfloat16 [96, 4, 8192], P(('groups', 'seq')), parts along dimension 0
There are 2 independent parts, one for each index of `groups`. A program takes and returns all parts, laid end to end along the dimension named above; an argument that names none is the same for every part. Nothing has to cross between parts.
Inputs may be any that keep to these rules, and one draw needn't show every extreme that they name: Block j of request r lies in row block_src[r, j] * 72 + block_slot[r, j] of latents; no two blocks of the part share a row; of the blocks of the requests that one device decodes, at most 5 lie on any one device. Only blocks j with j * 128 < lengths[r] are read. `place`: each decode row is taken by exactly one request; device i decodes the rows i * 3 to (i + 1) * 3 - 1. `lengths`: some request has exactly 3072 cached tokens.
All inputs are finite; a program needn't handle non-finite values.
Results may differ from a plain program's by a relative error of at most 0.012.
The roundings to bfloat16 on the way count: a program that leaves them out, or rounds other values in their place, can miss the bound.
Values may be sent and summed in bfloat16 or wider, within the bound.
A program may use at most 128 MiB of HBM per device.

v0:
```python
import jax
import jax.numpy as jnp
from jax import lax
from jax.sharding import PartitionSpec as P

HQ = 64
HK = 8
HD = 128
R = 256
BLOCK = 128
MAXB = 24
STEPS = 4


def project(latent_rows, weight):
    return jnp.dot(latent_rows, weight, preferred_element_type=jnp.float32).astype(jnp.bfloat16)


def attend(key_latent, value_latent, fresh, query, length, up_key, up_value):
    context = key_latent.shape[0]
    key_rows = project(key_latent, up_key)
    value_rows = project(value_latent, up_value)
    group = HQ // HK
    scale = HD ** (-0.5)
    query_heads = query.reshape(STEPS, HK, group, HD)
    fresh_keys = project(fresh[:, :R], up_key).reshape(STEPS, HK, HD)
    fresh_values = project(fresh[:, R:], up_value).reshape(STEPS, HK, HD)
    cached_scores = (
        jnp.einsum(
            "sgjd,tgd->gjst",
            query_heads,
            key_rows.reshape(context, HK, HD),
            preferred_element_type=jnp.float32,
        )
        * scale
    )
    fresh_scores = (
        jnp.einsum("sgjd,tgd->gjst", query_heads, fresh_keys, preferred_element_type=jnp.float32)
        * scale
    )
    cached_mask = jnp.arange(context, dtype=jnp.int32) < length
    step_ids = jnp.arange(STEPS, dtype=jnp.int32)
    fresh_mask = step_ids[None, :] <= step_ids[:, None]
    cached_scores = jnp.where(cached_mask, cached_scores, -jnp.inf)
    fresh_scores = jnp.where(fresh_mask, fresh_scores, -jnp.inf)
    row_max = jnp.maximum(jnp.max(cached_scores, axis=-1), jnp.max(fresh_scores, axis=-1))[
        ..., None
    ]
    cached_weights = jnp.exp(cached_scores - row_max)
    fresh_weights = jnp.exp(fresh_scores - row_max)
    denominator = jnp.sum(cached_weights, axis=-1) + jnp.sum(fresh_weights, axis=-1)
    mixed = jnp.einsum(
        "gjst,tgd->sgjd",
        cached_weights.astype(jnp.bfloat16),
        value_rows.reshape(context, HK, HD),
        preferred_element_type=jnp.float32,
    )
    mixed = mixed + jnp.einsum(
        "gjst,tgd->sgjd",
        fresh_weights.astype(jnp.bfloat16),
        fresh_values,
        preferred_element_type=jnp.float32,
    )
    result = mixed / jnp.transpose(denominator, (2, 0, 1))[..., None]
    return result.reshape(STEPS, HQ * HD).astype(jnp.bfloat16)


def local(latents, queries, new_latents, up_proj, lengths, place, block_src, block_slot):
    seq_devices = lax.axis_size("seq")
    device = lax.axis_index("seq")
    slot_count = latents.shape[0]
    local_count = queries.shape[0]
    request_count = place.shape[0]
    capacity = (slot_count + seq_devices - 1) // seq_devices
    up_weights = lax.all_gather(up_proj, "seq", axis=1, tiled=True)
    block_ids = jnp.arange(MAXB, dtype=jnp.int32)
    block_counts = (lengths + BLOCK - 1) // BLOCK
    is_live = block_ids[None, :] < block_counts[:, None]
    owners = place // local_count
    entry_ids = jnp.arange(request_count * MAXB, dtype=jnp.int32).reshape(request_count, MAXB)
    held_here = is_live & (block_src == device)
    slot_hits = (
        block_slot[:, :, None] == jnp.arange(slot_count, dtype=jnp.int32)[None, None, :]
    ) & held_here[:, :, None]
    slot_entry = jnp.sum(jnp.where(slot_hits, entry_ids[:, :, None] + 1, 0), axis=(0, 1)) - 1
    slot_used = slot_entry >= 0
    target_dev = owners[jnp.maximum(slot_entry, 0) // MAXB]
    earlier = (
        slot_used[None, :]
        & (target_dev[None, :] == target_dev[:, None])
        & (slot_entry[None, :] < slot_entry[:, None])
    )
    lane_rank = jnp.sum(earlier.astype(jnp.int32), axis=1)
    send_row = jnp.where(slot_used, target_dev * capacity + lane_rank, seq_devices * capacity)
    row_hits = send_row[:, None] == jnp.arange(seq_devices * capacity, dtype=jnp.int32)[None, :]
    source_slot = jnp.sum(
        jnp.where(row_hits, jnp.arange(slot_count, dtype=jnp.int32)[:, None], 0), axis=0
    )
    outgoing = jnp.take(latents, source_slot, axis=0)
    local_rows = device * local_count + jnp.arange(local_count, dtype=jnp.int32)
    requests = jnp.sum(
        jnp.where(
            place[None, :] == local_rows[:, None],
            jnp.arange(request_count, dtype=jnp.int32)[None, :],
            0,
        ),
        axis=1,
    )
    sources = block_src[requests].reshape(-1)
    live_local = is_live[requests].reshape(-1)
    entries = entry_ids[requests].reshape(-1)
    earlier_here = (
        live_local[None, :]
        & (sources[None, :] == sources[:, None])
        & (entries[None, :] < entries[:, None])
    )
    pick_rows = jnp.where(
        live_local, sources * capacity + jnp.sum(earlier_here.astype(jnp.int32), axis=1), 0
    )
    context = MAXB * BLOCK
    incoming = lax.all_to_all(outgoing, "seq", split_axis=0, concat_axis=0, tiled=True)
    gathered = jnp.take(incoming, pick_rows, axis=0).reshape(local_count, context, 2 * R)
    key_latent = gathered[:, :, :R]
    value_latent = gathered[:, :, R:]
    local_lengths = lengths[requests]

    def decode_one(items):
        return attend(
            items[0], items[1], items[2], items[3], items[4], up_weights[0], up_weights[1]
        )

    return lax.map(decode_one, (key_latent, value_latent, new_latents, queries, local_lengths))


def solution(mesh):
    return jax.shard_map(
        local,
        mesh=mesh,
        in_specs=(
            P(("groups", "seq"), None, None),
            P(("groups", "seq"), None, None),
            P(("groups", "seq"), None, None),
            P(None, "seq", None),
            P("groups"),
            P("groups"),
            P("groups", None),
            P("groups", None),
        ),
        out_specs=P(("groups", "seq"), None, None),
        check_vma=False,
    )
```

profile of v0, /device:TPU:13, one launch (start us, length us, event | category | flops | bytes accessed | tf_op | source)
XLA Modules:
  0.0 350.5 jit_solution(9547283987482918468)
XLA Ops:
  10.3 1.2 gather_fusion.3
  11.9 9.8 %gather_fusion.4 = bf16[80,128,512]{2,1,0:T(8,128)(2,1)} fusion(bf16[72,128,512]{2,1,0:T(8,128)(2,1)} %param.10, s32[1024]{0:T(1024)S(1)} %pad_clamp_fusion.1), kind=kCustom, calls=%fused_computation.4 | custom fusion | bytes 20971840 | tf_op jit(solution)/shard_map/jit(_take)/gather | solution.py:99
  21.7 10.1 %broadcast_select_fusion = bf16[80,128,512]{2,1,0:T(8,128)(2,1)} fusion(bf16[80,128,512]{2,1,0:T(8,128)(2,1)} %gather_fusion.4, pred[80]{0:T(512)(128)(4,1)S(1)} %compare_and_fusion.1), kind=kLoop, calls=%fused_computation.57 | loop fusion | flops 5242880 | bytes 20971600 | tf_op jit(solution)/shard_map/jit(_take)/select_n | solution.py:99
  31.8 6.7 %all-to-all-start = ((bf16[80,128,512]{2,1,0:T(8,128)(2,1)}), bf16[80,128,512]{2,1,0:T(8,128)(2,1)}, u32[]{:S(2)}, u32[]{:S(2)}) async-start(bf16[80,128,512]{2,1,0:T(8,128)(2,1)} %broadcast_select_fusion), calls=%async_computation | async-start | bytes 20971520 | tf_op jit(solution)/shard_map/all_to_all | solution.py:121
  42.6 229.5 %all-to-all-done = bf16[80,128,512]{2,1,0:T(8,128)(2,1)} async-done(((bf16[80,128,512]{2,1,0:T(8,128)(2,1)}), bf16[80,128,512]{2,1,0:T(8,128)(2,1)}, u32[]{:S(2)}, u32[]{:S(2)}) %all-to-all-start) | async-done | bytes 10485792 | tf_op jit(solution)/shard_map/all_to_all | solution.py:121
  272.0 9.9 %gather_fusion.5 = bf16[72,128,512]{2,1,0:T(8,128)(2,1)} fusion(bf16[80,128,512]{2,1,0:T(8,128)(2,1)} %all-to-all-done, s32[1024]{0:T(1024)S(1)} %pad_clamp_fusion), kind=kCustom, calls=%fused_computation.5 | custom fusion | bytes 18874656 | tf_op jit(solution)/shard_map/jit(_take)/gather | solution.py:122
  282.0 6.1 %bitcast_select_fusion = bf16[3,3072,512]{2,1,0:T(8,128)(2,1)S(1)} fusion(pred[3,3072]{1,0:T(4,128)(4,1)S(1)} %bitcast.154, bf16[3,3072,512]{2,1,0:T(8,128)(2,1)} %bitcast.153), kind=kLoop, calls=%fused_computation.58 | loop fusion | flops 4718592 | bytes 18883584 | tf_op jit(solution)/shard_map/jit(_take)/select_n | solution.py:122
  288.1 4.2 %fusion.54 = (bf16[3,3072,256]{2,1,0:T(8,128)(2,1)}, bf16[3,3072,256]{2,1,0:T(8,128)(2,1)}) fusion(bf16[3,3072,512]{2,1,0:T(8,128)(2,1)S(1)} %bitcast_select_fusion), kind=kLoop, calls=%fused_computation.104 | loop fusion | bytes 18874368 | tf_op jit(solution)/shard_map/slice | solution.py:123
  292.3 51.4 %while.10 = (s32[]{:T(128)}, bf16[3,4,8192]{2,1,0:T(4,128)(2,1)}, bf16[3,3072,256]{2,1,0:T(8,128)(2,1)}, bf16[2,256,1024]{2,1,0:T(8,128)(2,1)}, s32[3]{0:T(128)S...) while((s32[]{:T(128)}, bf16[3,4,8192]{2,1,0:T(4,128)(2,1)}, ...), condition=%wide.region_10.11_spmd, body=%wide.region_5.10_spmd.sunk | while | flops 3640509952 | bytes 40969348 | solution.py:132
  292.3 3.4 convolution_convert_fusion.7
  299.6 1.6 fusion.88
  301.9 3.4 convolution_convert_fusion.6
  305.2 2.1 fusion.89
  307.4 1.4 fusion.92
  309.4 3.4 convolution_convert_fusion.7
  316.7 1.6 fusion.88
  319.0 3.4 convolution_convert_fusion.6
  322.4 2.1 fusion.89
  324.5 1.4 fusion.92
  326.6 3.4 convolution_convert_fusion.7
  333.9 1.6 fusion.88
  336.1 3.4 convolution_convert_fusion.6
  339.5 2.1 fusion.89
  341.6 1.4 fusion.92
  (86 shorter events, 24.0 us)
Async XLA Ops:
  31.8 7.4 %copy-start.1 = (s32[48]{0:T(128)S(1)}, s32[48]{0:T(128)}, u32[]{:S(2)}) copy-start(s32[48]{0:T(128)} %param.15) | copy-start | bytes 580
  31.8 8.9 %copy-start = (s32[48]{0:T(128)S(1)}, s32[48]{0:T(128)}, u32[]{:S(2)}) copy-start(s32[48]{0:T(128)} %param.14) | copy-start | bytes 580
  31.8 240.3 %all-to-all-start = ((bf16[80,128,512]{2,1,0:T(8,128)(2,1)}), bf16[80,128,512]{2,1,0:T(8,128)(2,1)}, u32[]{:S(2)}, u32[]{:S(2)}) async-start(bf16[80,128,512]{2,1,0:T(8,128)(2,1)} %broadcast_select_fusion), calls=%async_computation | async-start | bytes 20971520 | tf_op jit(solution)/shard_map/all_to_all | solution.py:121
  38.4 253.9 %all-gather.2.cloned.1.call-start = ((), (), s32[]{:S(2)}) async-start(), calls=%async_computation.1 | async-start | bytes 1114112 | tf_op jit(solution)/shard_map/all_gather | solution.py:75
Sparse Core Ops, SparseCore 0:
  41.4 139.6 all-gather.1
where the time goes:
time: 352 us; the launch traced here: 351 us
  waiting for transfers between devices  230 us (65%)
  matrix products  38.6 us (11%)
  local copies, waits for them, and re-layouts  38.4 us (11%)
  other arithmetic  23 us (7%)
  between operations  13.5 us (4%)
  starting transfers between devices  6.88 us (2%)
    all_to_all x1, waiting for transfers between devices, local(): lax.all_to_all(outgoing, 'seq', split_axis=0, concat_axis=0, tiled=True)  229 us
    dot_general x6, matrix products, project(): jnp.dot(latent_rows, weight, preferred_element_type=jnp.float32)  20.1 us
    select_n x2, other arithmetic, local(): outgoing = jnp.take(latents, source_slot, axis=0)  10.1 us
    gather x1, local copies, waits for them, and re-layouts, local(): jnp.take(incoming, pick_rows, axis=0).reshape(local_count, context, 2 * R)  9.92 us
    gather x1, local copies, waits for them, and re-layouts, local(): outgoing = jnp.take(latents, source_slot, axis=0)  9.82 us
  transfers between devices with their start and end apart: 2, of which 1 were waited for; matrix products, arithmetic and copies ran while one was open for 7% of the time, Pallas kernels for 0%

commit v1 on v0

--- a/solution.py
+++ b/solution.py
@@ -1,6 +1,8 @@
 import jax
 import jax.numpy as jnp
 from jax import lax
+from jax.experimental import pallas as pl
+from jax.experimental.pallas import tpu as pltpu
 from jax.sharding import PartitionSpec as P
 
 HQ = 64
@@ -65,7 +67,7 @@
     return result.reshape(STEPS, HQ * HD).astype(jnp.bfloat16)
 
 
-def local(latents, queries, new_latents, up_proj, lengths, place, block_src, block_slot):
+def move_blocks(latents, queries, new_latents, up_proj, lengths, place, block_src, block_slot):
     seq_devices = lax.axis_size("seq")
     device = lax.axis_index("seq")
     slot_count = latents.shape[0]
@@ -132,6 +134,172 @@
     return lax.map(decode_one, (key_latent, value_latent, new_latents, queries, local_lengths))
 
 
+GROUP = HQ // HK
+ROWS = HQ * STEPS
+SCALE = HD ** (-0.5)
+CHUNK = 4
+NEG = float("-inf")
+
+
+def slot_plan(lengths, place, block_src, block_slot, device, slot_count):
+    starts = jnp.arange(MAXB, dtype=jnp.int32) * BLOCK
+    visible = jnp.clip(lengths[:, None] - starts[None, :], 0, BLOCK)
+    code = place[:, None] * 256 + visible
+    hits = (block_slot[:, :, None] == jnp.arange(slot_count, dtype=jnp.int32)) & (
+        block_src == device
+    )[:, :, None]
+    code = jnp.sum(jnp.where(hits, code[:, :, None], 0), axis=(0, 1))
+    return code // 256, code % 256
+
+
+def scores_kernel(row_ref, vis_ref, lat_ref, q_ref, up_ref, s_ref, m_ref):
+    step = pl.program_id(0)
+
+    @pl.when(step == 0)
+    def _():
+        m_ref[...] = jnp.full(m_ref.shape, NEG, jnp.float32)
+
+    lanes = lax.broadcasted_iota(jnp.int32, (ROWS, BLOCK), 1)
+    flat = lat_ref[...].reshape(CHUNK * BLOCK, R)
+    keys = project(flat, up_ref[...])
+    for c in range(CHUNK):
+        row = row_ref[step * CHUNK + c]
+        vis = vis_ref[step * CHUNK + c]
+
+        @pl.when(vis > 0)
+        def _():
+            parts = []
+            for g in range(HK):
+                parts.append(
+                    lax.dot_general(
+                        q_ref[row, g * 32 : (g + 1) * 32, :],
+                        keys[c * BLOCK : (c + 1) * BLOCK, g * HD : (g + 1) * HD],
+                        (((1,), (1,)), ((), ())),
+                        preferred_element_type=jnp.float32,
+                    )
+                )
+            s = jnp.concatenate(parts, axis=0) * SCALE
+            s = jnp.where(lanes < vis, s, NEG)
+            s_ref[c] = s
+            m = jnp.max(s, axis=1, keepdims=True)
+            m_ref[...] = jnp.where(lanes == row, jnp.maximum(m_ref[...], m), m_ref[...])
+
+
+def mix_kernel(row_ref, vis_ref, lat_ref, s_ref, m_ref, up_ref, o_ref, l_ref):
+    step = pl.program_id(0)
+
+    @pl.when(step == 0)
+    def _():
+        o_ref[...] = jnp.zeros(o_ref.shape, jnp.float32)
+        l_ref[...] = jnp.zeros(l_ref.shape, jnp.float32)
+
+    lanes = lax.broadcasted_iota(jnp.int32, (ROWS, BLOCK), 1)
+    flat = lat_ref[...].reshape(CHUNK * BLOCK, R)
+    vals = project(flat, up_ref[...])
+    for c in range(CHUNK):
+        row = row_ref[step * CHUNK + c]
+        vis = vis_ref[step * CHUNK + c]
+
+        @pl.when(vis > 0)
+        def _():
+            m = jnp.max(jnp.where(lanes == row, m_ref[...], NEG), axis=1, keepdims=True)
+            p = jnp.exp(s_ref[c] - m)
+            total = jnp.sum(p, axis=1, keepdims=True)
+            l_ref[...] = jnp.where(lanes == row, l_ref[...] + total, l_ref[...])
+            p = p.astype(jnp.bfloat16)
+            for g in range(HK):
+                o_ref[row, g * 32 : (g + 1) * 32, :] += jnp.dot(
+                    p[g * 32 : (g + 1) * 32],
+                    vals[c * BLOCK : (c + 1) * BLOCK, g * HD : (g + 1) * HD],
+                    preferred_element_type=jnp.float32,
+                )
+
+
+def whole(shape):
+    return pl.BlockSpec(shape, lambda i, *_: (0,) * len(shape))
+
+
+def local(latents, queries, new_latents, up_proj, lengths, place, block_src, block_slot):
+    slot_count = latents.shape[0]
+    count = queries.shape[0]
+    requests = place.shape[0]
+    if requests > BLOCK or slot_count % CHUNK:
+        return move_blocks(
+            latents, queries, new_latents, up_proj, lengths, place, block_src, block_slot
+        )
+    device = lax.axis_index("seq")
+    row, vis = slot_plan(lengths, place, block_src, block_slot, device, slot_count)
+    heads = queries.reshape(count, STEPS, HK, GROUP, HD).transpose(0, 2, 1, 3, 4)
+    heads = heads.reshape(count, ROWS, HD)
+    up = lax.all_gather(up_proj, "seq", axis=1, tiled=True)
+    q_all = lax.all_gather(heads, "seq", axis=0, tiled=True)
+    steps = slot_count // CHUNK
+    s, m = pl.pallas_call(
+        scores_kernel,
+        grid_spec=pltpu.PrefetchScalarGridSpec(
+            num_scalar_prefetch=2,
+            grid=(steps,),
+            in_specs=[
+                pl.BlockSpec((CHUNK, BLOCK, R), lambda i, *_: (i, 0, 0)),
+                whole((requests, ROWS, HD)),
+                pl.BlockSpec((None, R, HK * HD), lambda i, *_: (0, 0, 0)),
+            ],
+            out_specs=[
+                pl.BlockSpec((CHUNK, ROWS, BLOCK), lambda i, *_: (i, 0, 0)),
+                whole((ROWS, BLOCK)),
+            ],
+        ),
+        out_shape=[
+            jax.ShapeDtypeStruct((slot_count, ROWS, BLOCK), jnp.float32),
+            jax.ShapeDtypeStruct((ROWS, BLOCK), jnp.float32),
+        ],
+        compiler_params=pltpu.CompilerParams(vmem_limit_bytes=48 * 2**20),
+    )(row, vis, latents, q_all, up)
+    fresh_k = project(new_latents[:, :, :R], up[0]).reshape(count, STEPS, HK, HD)
+    fresh_v = project(new_latents[:, :, R:], up[1]).reshape(count, STEPS, HK, HD)
+    q_own = heads.reshape(count, HK, STEPS * GROUP, HD)
+    fs = jnp.einsum("bgrd,btgd->bgrt", q_own, fresh_k, preferred_element_type=jnp.float32) * SCALE
+    ok = jnp.arange(STEPS)[None, :] <= (jnp.arange(STEPS * GROUP) // GROUP)[:, None]
+    fs = jnp.where(ok, fs, NEG)
+    fm = jnp.max(fs, axis=-1).reshape(count, ROWS)
+    first = device * count
+    m = m[:, :requests].T
+    own = lax.dynamic_slice(m, (first, 0), (count, ROWS))
+    m = lax.dynamic_update_slice(m, jnp.maximum(own, fm), (first, 0))
+    m = lax.pmax(m, "seq")
+    own = lax.dynamic_slice(m, (first, 0), (count, ROWS)).reshape(count, HK, STEPS * GROUP)
+    m_cols = jnp.pad(m.T, ((0, 0), (0, BLOCK - requests)))
+    o, l = pl.pallas_call(
+        mix_kernel,
+        grid_spec=pltpu.PrefetchScalarGridSpec(
+            num_scalar_prefetch=2,
+            grid=(steps,),
+            in_specs=[
+                pl.BlockSpec((CHUNK, BLOCK, R), lambda i, *_: (i, 0, 1)),
+                pl.BlockSpec((CHUNK, ROWS, BLOCK), lambda i, *_: (i, 0, 0)),
+                whole((ROWS, BLOCK)),
+                pl.BlockSpec((None, R, HK * HD), lambda i, *_: (1, 0, 0)),
+            ],
+            out_specs=[whole((requests, ROWS, HD)), whole((ROWS, BLOCK))],
+        ),
+        out_shape=[
+            jax.ShapeDtypeStruct((requests, ROWS, HD), jnp.float32),
+            jax.ShapeDtypeStruct((ROWS, BLOCK), jnp.float32),
+        ],
+        compiler_params=pltpu.CompilerParams(vmem_limit_bytes=48 * 2**20),
+    )(row, vis, latents, s, m_cols, up)
+    o = lax.psum_scatter(o, "seq", scatter_dimension=0, tiled=True)
+    l = lax.psum_scatter(l[:, :requests].T, "seq", scatter_dimension=0, tiled=True)
+    fw = jnp.exp(fs - own[..., None])
+    l = l.reshape(count, HK, STEPS * GROUP) + jnp.sum(fw, axis=-1)
+    o = o.reshape(count, HK, STEPS * GROUP, HD) + jnp.einsum(
+        "bgrt,btgd->bgrd", fw.astype(jnp.bfloat16), fresh_v, preferred_element_type=jnp.float32
+    )
+    o = (o / l[..., None]).astype(jnp.bfloat16)
+    o = o.reshape(count, HK, STEPS, GROUP, HD).transpose(0, 2, 1, 3, 4)
+    return o.reshape(count, STEPS, HQ * HD)
+
+
 def solution(mesh):
     return jax.shard_map(
         local,

time: 352 us -> 310 us (0.88)
  the two profiles are of different devices: /device:TPU:13 before, /device:TPU:0 now
where the time goes in v1:
time: 310 us; the launch traced here: 308 us
  blocking collectives  120 us (39%)
  waiting for transfers between devices  104 us (34%)
  Pallas kernels  55.3 us (18%)
  between operations  13.9 us (4%)
  local copies, waits for them, and re-layouts  8.45 us (3%)
    pmax x1, blocking collectives, local(): m = lax.pmax(m, 'seq')  60.2 us
    unnamed x1, blocking collectives  59.8 us
    all_gather x1, waiting for transfers between devices, local(): q_all = lax.all_gather(heads, 'seq', axis=0, tiled=True)  44.8 us
    all_gather x1, waiting for transfers between devices, local(): up = lax.all_gather(up_proj, 'seq', axis=1, tiled=True)  37.2 us
    pallas_call x1, Pallas kernels, local(): pl.pallas_call(scores_kernel, grid_spec=pltpu.PrefetchScalarGridSpec(num_...  28 us
    pallas_call x1, Pallas kernels, local(): pl.pallas_call(mix_kernel, grid_spec=pltpu.PrefetchScalarGridSpec(num_sca...  27.3 us
    reduce_scatter x1, waiting for transfers between devices, local(): o = lax.psum_scatter(o, 'seq', scatter_dimension=0, tiled=True)  21.6 us
  transfers between devices with their start and end apart: 3, of which 3 were waited for; matrix products, arithmetic and copies ran while one was open for 3% of the time, Pallas kernels for 0%

profile of v1, /device:TPU:0, one launch (start us, length us, event | category | flops | bytes accessed | tf_op | source)
XLA Modules:
  0.0 308.0 jit_solution(5012736873010526505)
XLA Ops:
  6.5 0.7 all-gather.5.cloned.1.call-update
  7.3 1.1 reshape.100
  8.5 0.7 copy.35
  9.2 0.7 broadcast_compare_fusion
  10.1 0.8 copy.33
  10.9 0.7 broadcast_multiply_fusion
  11.5 0.7 clamp_add_fusion
  12.3 0.7 select_reduce_fusion
  13.0 37.2 %all-gather.5.cloned.1.call-done.up_ref = bf16[2,256,1024]{2,1,0:T(8,128)(2,1)} async-done(((bf16[2,16,1024]{2,1,0:T(8,128)(2,1)}), bf16[2,256,1024]{2,1,0:T(8,128)(2,1)}) %all-gather.5.cloned.1.call-update) | async-done | bytes 1048592 | tf_op jit(solution)/shard_map/all_gather | solution.py:234
  50.2 1.4 fusion.19
  51.7 0.1 copy.37
  51.8 44.8 %all-gather.3.cloned.1.call-done.q_ref = bf16[48,256,128]{2,1,0:T(8,128)(2,1)} async-done(((bf16[3,256,128]{2,1,0:T(8,128)(2,1)}), bf16[48,256,128]{2,1,0:T(8,128)(2,1)}) %all-gather.3.cloned.1.call-update) | async-done | bytes 3145744 | tf_op jit(solution)/shard_map/all_gather | solution.py:235
  96.7 1.2 copy-done
  97.9 1.9 copy-done.2
  99.8 28.0 %shard_map.82 = (f32[72,256,128]{2,1,0:T(8,128)}, f32[256,128]{1,0:T(8,128)S(1)}) custom-call(s32[72]{0:T(128)S(1)} %get-tuple-element.16.row_ref, s32[72]{0:T(128)S(1)} %get-tuple-element.15.vis_ref, bf16[72,128,512]{2,1,0:T(8,128)(2,1)} %lat_ref.3, bf16[48,256,128]{2,1,0:T(8,128)(2,1)S(1)} %copy-done.2, bf16[2,256,1024]{2,1,0:T(8,128)(2,1)S(1)} %copy-done), custom_call_target="tpu_custom_call" | custom-call | tf_op jit(solution)/shard_map/pallas_call | solution.py:237
  127.9 0.6 dynamic_update_slice.3
  128.5 60.2 %pmax.7 = f32[48,256]{0,1:T(8,128)S(1)} all-reduce(f32[48,256]{0,1:T(8,128)S(1)} %dynamic_update_slice.3), channel_id=1, replica_groups=mesh['groups'=2,'seq'=16] {'seq'}, use_global_device_ids=true, to_apply=%region_2.3 | all-reduce | flops 12288 | bytes 98304 | tf_op jit(solution)/shard_map/pmax | solution.py:269
  188.8 27.3 %shard_map.83 = (f32[48,256,128]{2,1,0:T(8,128)}, f32[256,128]{1,0:T(8,128)S(1)}) custom-call(s32[72]{0:T(128)S(1)} %get-tuple-element.16.row_ref, s32[72]{0:T(128)S(1)} %get-tuple-element.15.vis_ref, bf16[72,128,512]{2,1,0:T(8,128)(2,1)} %lat_ref.3, f32[72,256,128]{2,1,0:T(8,128)} %get-tuple-element.9.s_ref, f32[256,128]{1,0:T(8,128)S(1)} %pad.4.m_ref, ...), custom_call_target="tpu_custom_call" | custom-call | tf_op jit(solution)/shard_map/pallas_call | solution.py:272
  216.1 0.6 dynamic-slice.4
  217.5 0.1 copy.42
  217.6 59.8 %all-reduce.1 = f32[48,256]{0,1:T(8,128)S(1)} all-reduce(f32[48,256]{0,1:T(8,128)S(1)} %slice_bitcast_fusion.6), channel_id=3, replica_groups=mesh['groups'=2,'seq'=16] {'seq'}, use_global_device_ids=true, to_apply=%region_4.5.clone | all-reduce | flops 12288 | bytes 98304
  277.8 21.6 %reduce-scatter.3.cloned.1.call-done = f32[3,256,128]{2,1,0:T(8,128)} async-done(((f32[48,256,128]{2,1,0:T(8,128)}), f32[3,256,128]{2,1,0:T(8,128)}) %reduce-scatter.3.cloned.1.call-update) | async-done | bytes 393232 | tf_op jit(solution)/shard_map/reduce_scatter | solution.py:291
  299.3 1.4 fusion.2
  300.8 0.7 reshape.108
  (28 shorter events, 0.8 us)
Async XLA Ops:
  6.5 43.7 %all-gather.5.cloned.1.call-start = ((), (), s32[]{:S(2)}) async-start(), calls=%async_computation.2 | async-start | bytes 1114112 | tf_op jit(solution)/shard_map/all_gather | solution.py:234
  7.3 89.4 %all-gather.3.cloned.1.call-start = ((), (), s32[]{:S(2)}) async-start(), calls=%async_computation.1 | async-start | bytes 3342336 | tf_op jit(solution)/shard_map/all_gather | solution.py:235
  9.2 290.1 %reduce-scatter.3.cloned.1.call-start = ((), (), s32[]{:S(2)}) async-start(), calls=%async_computation.3 | async-start | bytes 6684672 | tf_op jit(solution)/shard_map/reduce_scatter | solution.py:291
  96.7 1.2 copy-start
  97.9 1.9 copy-start.2
  99.8 89.0 %copy-start.1 = (bf16[2,256,1024]{2,1,0:T(8,128)(2,1)S(1)}, bf16[2,256,1024]{2,1,0:T(8,128)(2,1)}, u32[]{:S(2)}) copy-start(bf16[2,256,1024]{2,1,0:T(8,128)(2,1)} %all-gather.5.cloned.1.call-done.up_ref) | copy-start | bytes 3145732
  188.8 27.4 %copy-start.4 = (u32[32]{0:T(128)S(1)}, u32[32]{0:T(128)}, u32[]{:S(2)}) copy-start(u32[32]{0:T(128)} %constant.69) | copy-start | bytes 388
  188.8 110.5 %copy-start.3 = (bf16[3,4,512]{2,1,0:T(4,128)(2,1)S(1)}, bf16[3,4,512]{2,1,0:T(4,128)(2,1)}, u32[]{:S(2)}) copy-start(bf16[3,4,512]{2,1,0:T(4,128)(2,1)} %param.10) | copy-start | bytes 36868
Sparse Core Ops, SparseCore 0:
  9.5 40.6 all-gather.4
  52.5 44.0 all-gather.2
  216.2 83.0 reduce-scatter.2

commit v2 on v1

--- a/solution.py
+++ b/solution.py
@@ -185,7 +185,7 @@
             m_ref[...] = jnp.where(lanes == row, jnp.maximum(m_ref[...], m), m_ref[...])
 
 
-def mix_kernel(row_ref, vis_ref, lat_ref, s_ref, m_ref, up_ref, o_ref, l_ref):
+def mix_kernel(row_ref, vis_ref, lat_ref, s_ref, m_ref, up_ref, out_ref, l_ref, o_ref):
     step = pl.program_id(0)
 
     @pl.when(step == 0)
@@ -214,6 +214,247 @@
                     preferred_element_type=jnp.float32,
                 )
 
+    @pl.when(step == pl.num_programs(0) - 1)
+    def _():
+        for r in range(o_ref.shape[0]):
+            out_ref[r] = o_ref[r].astype(jnp.bfloat16)
+
+
+NZ, NY, NC = 4, 2, 2
+
+
+def coords():
+    me = lax.axis_index("seq")
+    return me // 4, (me // 2) % 2, me % 2
+
+
+def at(z, y, c):
+    return z * 4 + y * 2 + c
+
+
+def meet(z, y, c):
+    barrier = pltpu.get_barrier_semaphore()
+    for d in (at(z, 1 - y, c), at(z, y, 1 - c), *[at((z + k) % NZ, y, c) for k in (1, 2, 3)]):
+        pl.semaphore_signal(
+            barrier, inc=1, device_id={"seq": d}, device_id_type=pl.DeviceIdType.MESH
+        )
+    pl.semaphore_wait(barrier, 5)
+
+
+def send(src, dst, send_sem, recv_sem, dev):
+    return pltpu.make_async_remote_copy(
+        src_ref=src,
+        dst_ref=dst,
+        send_sem=send_sem,
+        recv_sem=recv_sem,
+        device_id={"seq": dev},
+        device_id_type=pl.DeviceIdType.MESH,
+    )
+
+
+def gather_kernel(q_ref, up_ref, q_out, up_out, ys, yr, zs, zr, cs, cr, own):
+    z, y, c = coords()
+    meet(z, y, c)
+    depth = up_ref.shape[1]
+
+    def shard(d):
+        rows = pl.ds(pl.multiple_of(d * depth, depth), depth)
+        return up_out.at[:, rows, :], q_out.at[d]
+
+    def copies(source, d, ssem, rsem, dev):
+        return [
+            send(s, t, ssem.at[n], rsem.at[n], dev)
+            for n, (s, t) in enumerate(zip(source, shard(d)))
+        ]
+
+    me = at(z, y, c)
+    mine = (up_ref, q_ref)
+    local_copies = [
+        pltpu.make_async_copy(s, t, own.at[n]) for n, (s, t) in enumerate(zip(mine, shard(me)))
+    ]
+    y_dev, c_dev = at(z, 1 - y, c), at(z, y, 1 - c)
+    y_send, z_send, c_send = [], [], []
+    y_send += copies(mine, me, ys.at[0], yr.at[0], y_dev)
+    for k in (1, 2, 3):
+        z_send += copies(mine, me, zs.at[k], zr.at[k], at((z + k) % NZ, y, c))
+    c_send += copies(mine, me, cs.at[0], cr.at[0], c_dev)
+    for cp in y_send + z_send + c_send + local_copies:
+        cp.start()
+
+    def arrived(d, sem):
+        for n, t in enumerate(shard(d)):
+            send(t, t, own.at[n], sem.at[n], y_dev).wait_recv()
+
+    def forward(d, ssem, rsem, dev):
+        more = copies(shard(d), d, ssem, rsem, dev)
+        for cp in more:
+            cp.start()
+        return more
+
+    arrived(at(z, 1 - y, c), yr.at[0])
+    c_send += forward(at(z, 1 - y, c), cs.at[4], cr.at[4], c_dev)
+    for k in (1, 2, 3):
+        d = at((z - k + NZ) % NZ, y, c)
+        arrived(d, zr.at[k])
+        y_send += forward(d, ys.at[k], yr.at[k], y_dev)
+        c_send += forward(d, cs.at[k], cr.at[k], c_dev)
+    for k in (1, 2, 3):
+        d = at((z - k + NZ) % NZ, 1 - y, c)
+        arrived(d, yr.at[k])
+        c_send += forward(d, cs.at[4 + k], cr.at[4 + k], c_dev)
+    for k in range(NZ):
+        for w in range(NY):
+            arrived(at((z - k + NZ) % NZ, (y + w) % NY, 1 - c), cr.at[4 * w + k])
+    for cp in y_send + z_send + c_send:
+        cp.wait_send()
+    for cp in local_copies:
+        cp.wait()
+
+
+def gather(heads, up_proj):
+    count, rows, width = heads.shape
+    two, depth, cols = up_proj.shape
+    n = NZ * NY * NC
+    hbm = pl.BlockSpec(memory_space=pl.ANY)
+    dma = pltpu.SemaphoreType.DMA
+    return pl.pallas_call(
+        gather_kernel,
+        in_specs=[hbm, hbm],
+        out_specs=[hbm, hbm],
+        out_shape=[
+            jax.ShapeDtypeStruct((n, count, rows, width), heads.dtype),
+            jax.ShapeDtypeStruct((two, n * depth, cols), up_proj.dtype),
+        ],
+        scratch_shapes=[dma((4, 2))] * 4 + [dma((8, 2))] * 2 + [dma((2,))],
+        compiler_params=pltpu.CompilerParams(collective_id=0, has_side_effects=True),
+    )(heads, up_proj)
+
+
+def max_kernel(m_ref, out_ref, buf, stage, ss, rs):
+    z, y, c = coords()
+    meet(z, y, c)
+    stage[0] = m_ref[...]
+    for n, dev in ((0, at(z, y, 1 - c)), (1, at(z, 1 - y, c))):
+        cp = send(stage.at[n], buf.at[n], ss.at[n], rs.at[n], dev)
+        cp.start()
+        cp.wait()
+        stage[n + 1] = jnp.maximum(stage[n], buf[n])
+    cps = [
+        send(stage.at[2], buf.at[1 + k], ss.at[1 + k], rs.at[1 + k], at((z + k) % NZ, y, c))
+        for k in (1, 2, 3)
+    ]
+    for cp in cps:
+        cp.start()
+    for cp in cps:
+        cp.wait()
+    out_ref[...] = jnp.maximum(jnp.maximum(stage[2], buf[2]), jnp.maximum(buf[3], buf[4]))
+
+
+def global_max(m):
+    vmem = pl.BlockSpec(memory_space=pltpu.VMEM)
+    dma = pltpu.SemaphoreType.DMA
+    return pl.pallas_call(
+        max_kernel,
+        in_specs=[vmem],
+        out_specs=vmem,
+        out_shape=jax.ShapeDtypeStruct(m.shape, m.dtype),
+        scratch_shapes=[
+            pltpu.VMEM((5,) + m.shape, m.dtype),
+            pltpu.VMEM((3,) + m.shape, m.dtype),
+            dma((5,)),
+            dma((5,)),
+        ],
+        compiler_params=pltpu.CompilerParams(collective_id=1, has_side_effects=True),
+    )(m)
+
+
+def scatter_kernel(o_ref, l_ref, o_out, l_out, cb, cl, yb, yl, yi, yj, zb, zl, zi, zj, cs, cr, ys, yr, zs, zr):
+    z, y, c = coords()
+    meet(z, y, c)
+    y_dev, c_dev = at(z, 1 - y, c), at(z, y, 1 - c)
+    order = [(z + 1) % NZ, (z + 2) % NZ, (z + 3) % NZ, z]
+    sends = []
+
+    def pair(so, sl, to, tl, ssem, rsem, dev):
+        cps = [
+            send(so, to, ssem.at[0], rsem.at[0], dev),
+            send(sl, tl, ssem.at[1], rsem.at[1], dev),
+        ]
+        for cp in cps:
+            cp.start()
+        sends.extend(cps)
+        return cps
+
+    c_in = {}
+    for w in (1, 0):
+        for k in range(NZ):
+            d = at(order[k], (y + w) % NY, 1 - c)
+            i = 4 * w + k
+            c_in[w, k] = pair(
+                o_ref.at[d], l_ref.at[d], cb.at[i], cl.at[i], cs.at[i], cr.at[i], c_dev
+            )
+    f32 = jnp.float32
+    y_in = []
+    for k in range(NZ):
+        for cp in c_in[1, k]:
+            cp.wait_recv()
+        d = at(order[k], 1 - y, c)
+        yb[k] = (o_ref[d].astype(f32) + cb[4 + k].astype(f32)).astype(jnp.bfloat16)
+        yl[k] = l_ref[d] + cl[4 + k]
+        y_in.append(
+            pair(yb.at[k], yl.at[k], yi.at[k], yj.at[k], ys.at[k], yr.at[k], y_dev)
+        )
+    z_in = []
+    for k in range(NZ):
+        for cp in c_in[0, k] + y_in[k]:
+            cp.wait_recv()
+        d = at(order[k], y, c)
+        o = o_ref[d].astype(f32) + cb[k].astype(f32) + yi[k].astype(f32)
+        l = l_ref[d] + cl[k] + yj[k]
+        if k < NZ - 1:
+            zb[k] = o.astype(jnp.bfloat16)
+            zl[k] = l
+            z_in.append(
+                pair(
+                    zb.at[k], zl.at[k], zi.at[k], zj.at[k], zs.at[k], zr.at[k], at(order[k], y, c)
+                )
+            )
+        else:
+            o_out[...] = o
+            l_out[...] = l
+    for k in range(NZ - 1):
+        for cp in z_in[k]:
+            cp.wait_recv()
+        o_out[...] += zi[k].astype(f32)
+        l_out[...] += zj[k]
+    for cp in sends:
+        cp.wait_send()
+
+
+def scatter(o, l):
+    n, rows, width = o.shape
+    lr, lw = l.shape[1:]
+    vmem = pl.BlockSpec(memory_space=pltpu.VMEM)
+    dma = pltpu.SemaphoreType.DMA
+
+    def bufs(k):
+        return [pltpu.VMEM((k, rows, width), o.dtype), pltpu.VMEM((k, lr, lw), l.dtype)]
+
+    return pl.pallas_call(
+        scatter_kernel,
+        in_specs=[vmem, vmem],
+        out_specs=[vmem, vmem],
+        out_shape=[
+            jax.ShapeDtypeStruct((rows, width), jnp.float32),
+            jax.ShapeDtypeStruct((lr, lw), jnp.float32),
+        ],
+        scratch_shapes=bufs(8) + bufs(4) + bufs(4) + bufs(3) + bufs(3)
+        + [dma((8, 2))] * 2 + [dma((4, 2))] * 2 + [dma((3, 2))] * 2,
+        compiler_params=pltpu.CompilerParams(
+            collective_id=2, has_side_effects=True, vmem_limit_bytes=40 * 2**20
+        ),
+    )(o, l)
+
 
 def whole(shape):
     return pl.BlockSpec(shape, lambda i, *_: (0,) * len(shape))
@@ -223,7 +464,7 @@
     slot_count = latents.shape[0]
     count = queries.shape[0]
     requests = place.shape[0]
-    if requests > BLOCK or slot_count % CHUNK:
+    if lax.axis_size("seq") != 16 or requests > BLOCK or slot_count % CHUNK:
         return move_blocks(
             latents, queries, new_latents, up_proj, lengths, place, block_src, block_slot
         )
@@ -231,8 +472,8 @@
     row, vis = slot_plan(lengths, place, block_src, block_slot, device, slot_count)
     heads = queries.reshape(count, STEPS, HK, GROUP, HD).transpose(0, 2, 1, 3, 4)
     heads = heads.reshape(count, ROWS, HD)
-    up = lax.all_gather(up_proj, "seq", axis=1, tiled=True)
-    q_all = lax.all_gather(heads, "seq", axis=0, tiled=True)
+    q_all, up = gather(heads, up_proj)
+    q_all = q_all.reshape(requests, ROWS, HD)
     steps = slot_count // CHUNK
     s, m = pl.pallas_call(
         scores_kernel,
@@ -266,7 +507,7 @@
     m = m[:, :requests].T
     own = lax.dynamic_slice(m, (first, 0), (count, ROWS))
     m = lax.dynamic_update_slice(m, jnp.maximum(own, fm), (first, 0))
-    m = lax.pmax(m, "seq")
+    m = global_max(m)
     own = lax.dynamic_slice(m, (first, 0), (count, ROWS)).reshape(count, HK, STEPS * GROUP)
     m_cols = jnp.pad(m.T, ((0, 0), (0, BLOCK - requests)))
     o, l = pl.pallas_call(
@@ -281,15 +522,18 @@
                 pl.BlockSpec((None, R, HK * HD), lambda i, *_: (1, 0, 0)),
             ],
             out_specs=[whole((requests, ROWS, HD)), whole((ROWS, BLOCK))],
+            scratch_shapes=[pltpu.VMEM((requests, ROWS, HD), jnp.float32)],
         ),
         out_shape=[
-            jax.ShapeDtypeStruct((requests, ROWS, HD), jnp.float32),
+            jax.ShapeDtypeStruct((requests, ROWS, HD), jnp.bfloat16),
             jax.ShapeDtypeStruct((ROWS, BLOCK), jnp.float32),
         ],
         compiler_params=pltpu.CompilerParams(vmem_limit_bytes=48 * 2**20),
     )(row, vis, latents, s, m_cols, up)
-    o = lax.psum_scatter(o, "seq", scatter_dimension=0, tiled=True)
-    l = lax.psum_scatter(l[:, :requests].T, "seq", scatter_dimension=0, tiled=True)
+    devices = lax.axis_size("seq")
+    o, l = scatter(
+        o.reshape(devices, count * ROWS, HD), l[:, :requests].T.reshape(devices, count, ROWS)
+    )
     fw = jnp.exp(fs - own[..., None])
     l = l.reshape(count, HK, STEPS * GROUP) + jnp.sum(fw, axis=-1)
     o = o.reshape(count, HK, STEPS * GROUP, HD) + jnp.einsum(

time: 310 us -> 158 us (0.51)
  blocking collectives: 120 us -> 0 us
  waiting for transfers between devices: 104 us -> 0 us
  Pallas kernels: 55.3 us -> 139 us
  between operations: 13.9 us -> 0.19 us
  local copies, waits for them, and re-layouts: 8.45 us -> 13 us
    pallas_call x0 -> x3, Pallas kernels: none -> 88 us  [the longest x1 39 us: gather(): pl.pallas_call(gather_kernel, in_specs=[hbm, hbm], out_specs=[hbm, hbm],...]
    all_gather x2 -> x0, waiting for transfers between devices: 82.1 us -> none  [the longest x1 44.8 us: local(): q_all = lax.all_gather(heads, 'seq', axis=0, tiled=True)]
    pmax x1 -> x0, blocking collectives: 60.2 us -> none  [local(): m = lax.pmax(m, 'seq')]
    unnamed x1 -> x0, blocking collectives: 59.8 us -> none
    reduce_scatter x1 -> x0, waiting for transfers between devices: 21.6 us -> none  [local(): o = lax.psum_scatter(o, 'seq', scatter_dimension=0, tiled=True)]
    unnamed x13 -> x15, local copies, waits for them, and re-layouts: 4.59 us -> 8.05 us
    pallas_call x1, Pallas kernels: 27.3 us -> 23.9 us  [local(): pl.pallas_call(mix_kernel, grid_spec=pltpu.PrefetchScalarGridSpec(num_sca...]
  transfers between devices with their start and end apart: 3 -> 0, of which waited for: 3 -> 0; matrix products, arithmetic and copies ran while one was open for 3% -> 0% of each run, Pallas kernels for 0% -> 0%
where the time goes in v2:
time: 158 us; the launch traced here: 156 us
  Pallas kernels  139 us (88%)
  local copies, waits for them, and re-layouts  13 us (8%)
  other arithmetic  2.89 us (2%)
  matrix products  1.81 us (1%)
    pallas_call x1, Pallas kernels, gather(): pl.pallas_call(gather_kernel, in_specs=[hbm, hbm], out_specs=[hbm, hbm],...  39 us
    pallas_call x1, Pallas kernels, scatter(): pl.pallas_call(scatter_kernel, in_specs=[vmem, vmem], out_specs=[vmem, vm...  29.9 us
    pallas_call x1, Pallas kernels, local(): pl.pallas_call(scores_kernel, grid_spec=pltpu.PrefetchScalarGridSpec(num_...  26.6 us
    pallas_call x1, Pallas kernels, local(): pl.pallas_call(mix_kernel, grid_spec=pltpu.PrefetchScalarGridSpec(num_sca...  23.9 us
    pallas_call x1, Pallas kernels, global_max(): pl.pallas_call(max_kernel, in_specs=[vmem], out_specs=vmem, out_shape=jax...  19.2 us
    unnamed x15, local copies, waits for them, and re-layouts  8.05 us

profile of v2, /device:TPU:0, one launch (start us, length us, event | category | flops | bytes accessed | tf_op | source)
XLA Modules:
  0.0 156.4 jit_solution(8324414318018351286)
XLA Ops:
  0.0 0.7 broadcast_multiply_fusion
  0.7 0.7 broadcast_compare_fusion
  1.4 0.1 copy.28
  1.5 0.7 clamp_add_fusion
  2.2 0.8 copy.27
  3.0 0.7 select_reduce_fusion
  3.7 1.1 reshape.109
  4.9 0.7 copy.29
  5.6 39.0 %shard_map.82 = (bf16[16,3,256,128]{3,2,1,0:T(8,128)(2,1)}, bf16[2,256,1024]{2,1,0:T(8,128)(2,1)}) custom-call(bf16[3,256,128]{2,1,0:T(8,128)(2,1)} %bitcast.58, bf16[2,16,1024]{2,1,0:T(8,128)(2,1)} %up_ref.1), custom_call_target="tpu_custom_call" | custom-call | tf_op jit(solution)/shard_map/pallas_call | solution.py:320
  44.6 1.4 fusion.27
  46.1 1.2 copy-done
  47.3 1.9 %copy-done.4 = bf16[16,3,256,128]{3,2,1,0:T(8,128)(2,1)S(1)} copy-done((bf16[16,3,256,128]{3,2,1,0:T(8,128)(2,1)S(1)}, bf16[16,3,256,128]{3,2,1,0:T(8,128)(2,1)}, u32[]{:S(2)}) %copy-start.4) | copy-done | bytes 3145752
  49.2 26.6 %shard_map.83 = (f32[72,256,128]{2,1,0:T(8,128)}, f32[256,128]{1,0:T(8,128)S(1)}) custom-call(s32[72]{0:T(128)S(1)} %get-tuple-element.24.row_ref, s32[72]{0:T(128)S(1)} %get-tuple-element.23.vis_ref, bf16[72,128,512]{2,1,0:T(8,128)(2,1)} %lat_ref.3, bf16[48,256,128]{2,1,0:T(8,128)(2,1)S(1)} %bitcast.56, bf16[2,256,1024]{2,1,0:T(8,128)(2,1)S(1)} %copy-done), custom_call_target="tpu_custom_call" | custom-call | tf_op jit(solution)/shard_map/pallas_call | solution.py:478
  76.0 0.2 dynamic_update_slice.3.m_ref
  76.1 0.6 copy-done.5
  76.8 19.2 %shard_map.84 = f32[48,256]{1,0:T(8,128)} custom-call(f32[48,256]{1,0:T(8,128)} %copy-done.5), custom_call_target="tpu_custom_call" | custom-call | tf_op jit(solution)/shard_map/pallas_call | solution.py:356
  96.0 0.7 constant_dynamic-slice_fusion
  96.8 0.9 copy.32
  97.8 23.9 %shard_map.85 = (bf16[48,256,128]{2,1,0:T(8,128)(2,1)S(1)}, f32[256,128]{1,0:T(8,128)S(1)}) custom-call(s32[72]{0:T(128)S(1)} %get-tuple-element.24.row_ref, s32[72]{0:T(128)S(1)} %get-tuple-element.23.vis_ref, bf16[72,128,512]{2,1,0:T(8,128)(2,1)} %lat_ref.3, f32[72,256,128]{2,1,0:T(8,128)} %get-tuple-element.15.s_ref, f32[256,128]{1,0:T(8,128)S(1)} %pad.4.m_ref, ...), custom_call_target="tpu_custom_call" | custom-call | tf_op jit(solution)/shard_map/pallas_call | solution.py:513
  121.6 1.6 %copy-done.2 = bf16[48,256,128]{2,1,0:T(8,128)(2,1)} copy-done((bf16[48,256,128]{2,1,0:T(8,128)(2,1)}, bf16[48,256,128]{2,1,0:T(8,128)(2,1)S(1)}, u32[]{:S(2)}) %copy-start.2) | copy-done | bytes 3145752
  123.4 1.9 %copy-done.3 = bf16[48,256,128]{2,1,0:T(8,128)(2,1)S(1)} copy-done((bf16[48,256,128]{2,1,0:T(8,128)(2,1)S(1)}, bf16[48,256,128]{2,1,0:T(8,128)(2,1)}, u32[]{:S(2)}) %copy-start.3) | copy-done | bytes 3145752
  125.3 29.9 %shard_map.86 = (f32[768,128]{1,0:T(8,128)S(1)}, f32[3,256]{1,0:T(4,128)S(1)}) custom-call(bf16[16,768,128]{2,1,0:T(8,128)(2,1)S(1)} %bitcast.55, f32[16,3,256]{2,1,0:T(4,128)S(1)} %reshape.115.l_ref), custom_call_target="tpu_custom_call" | custom-call | tf_op jit(solution)/shard_map/pallas_call | solution.py:443
  155.3 0.4 fusion.2
  155.7 0.7 reshape.120
  (26 shorter events, 0.6 us)
Async XLA Ops:
  46.1 1.2 copy-start
  47.3 1.9 %copy-start.4 = (bf16[16,3,256,128]{3,2,1,0:T(8,128)(2,1)S(1)}, bf16[16,3,256,128]{3,2,1,0:T(8,128)(2,1)}, u32[]{:S(2)}) copy-start(bf16[16,3,256,128]{3,2,1,0:T(8,128)(2,1)} %get-tuple-element.13) | copy-start | bytes 9437188
  49.2 48.5 %copy-start.1 = (bf16[2,256,1024]{2,1,0:T(8,128)(2,1)S(1)}, bf16[2,256,1024]{2,1,0:T(8,128)(2,1)}, u32[]{:S(2)}) copy-start(bf16[2,256,1024]{2,1,0:T(8,128)(2,1)} %get-tuple-element.14.up_ref) | copy-start | bytes 3145732
  76.1 0.6 copy-start.5
  97.7 57.5 %copy-start.6 = (bf16[3,4,512]{2,1,0:T(4,128)(2,1)S(1)}, bf16[3,4,512]{2,1,0:T(4,128)(2,1)}, u32[]{:S(2)}) copy-start(bf16[3,4,512]{2,1,0:T(4,128)(2,1)} %param.10) | copy-start | bytes 36868
  121.6 1.7 %copy-start.2 = (bf16[48,256,128]{2,1,0:T(8,128)(2,1)}, bf16[48,256,128]{2,1,0:T(8,128)(2,1)S(1)}, u32[]{:S(2)}) copy-start(bf16[48,256,128]{2,1,0:T(8,128)(2,1)S(1)} %get-tuple-element.17) | copy-start | bytes 9437188
  123.4 1.9 %copy-start.3 = (bf16[48,256,128]{2,1,0:T(8,128)(2,1)S(1)}, bf16[48,256,128]{2,1,0:T(8,128)(2,1)}, u32[]{:S(2)}) copy-start(bf16[48,256,128]{2,1,0:T(8,128)(2,1)} %copy-done.2) | copy-start | bytes 9437188

commit v3 on v2

--- a/solution.py
+++ b/solution.py
@@ -145,14 +145,22 @@
     starts = jnp.arange(MAXB, dtype=jnp.int32) * BLOCK
     visible = jnp.clip(lengths[:, None] - starts[None, :], 0, BLOCK)
     code = place[:, None] * 256 + visible
-    hits = (block_slot[:, :, None] == jnp.arange(slot_count, dtype=jnp.int32)) & (
-        block_src == device
-    )[:, :, None]
+    slots = jnp.arange(slot_count, dtype=jnp.int32)
+    hits = (block_slot[:, :, None] == slots) & (block_src == device)[:, :, None]
     code = jnp.sum(jnp.where(hits, code[:, :, None], 0), axis=(0, 1))
-    return code // 256, code % 256
-
-
-def scores_kernel(row_ref, vis_ref, lat_ref, q_ref, up_ref, s_ref, m_ref):
+    live = code % 256 > 0
+    ahead = (live[None, :] & ~live[:, None]) | (
+        (live[None, :] == live[:, None]) & (slots[None, :] < slots[:, None])
+    )
+    rank = jnp.sum(ahead.astype(jnp.int32), axis=1)
+    packed = code * 256 + slots
+    packed = jnp.sum(jnp.where(rank[:, None] == slots[None, :], packed[:, None], 0), axis=0)
+    return packed % 256, packed // 65536, (packed // 256) % 256
+
+
+def scores_kernel(slot_ref, row_ref, vis_ref, *refs):
+    keys = refs[:CHUNK]
+    q_ref, s_ref, m_ref = refs[CHUNK:]
     step = pl.program_id(0)
 
     @pl.when(step == 0)
@@ -160,20 +168,19 @@
         m_ref[...] = jnp.full(m_ref.shape, NEG, jnp.float32)
 
     lanes = lax.broadcasted_iota(jnp.int32, (ROWS, BLOCK), 1)
-    flat = lat_ref[...].reshape(CHUNK * BLOCK, R)
-    keys = project(flat, up_ref[...])
-    for c in range(CHUNK):
-        row = row_ref[step * CHUNK + c]
-        vis = vis_ref[step * CHUNK + c]
-
-        @pl.when(vis > 0)
-        def _():
+
+    @pl.when(vis_ref[step * CHUNK] > 0)
+    def _():
+        best = m_ref[...]
+        for c in range(CHUNK):
+            row = row_ref[step * CHUNK + c]
+            vis = vis_ref[step * CHUNK + c]
             parts = []
             for g in range(HK):
                 parts.append(
                     lax.dot_general(
                         q_ref[row, g * 32 : (g + 1) * 32, :],
-                        keys[c * BLOCK : (c + 1) * BLOCK, g * HD : (g + 1) * HD],
+                        keys[c][:, g * HD : (g + 1) * HD],
                         (((1,), (1,)), ((), ())),
                         preferred_element_type=jnp.float32,
                     )
@@ -182,10 +189,13 @@
             s = jnp.where(lanes < vis, s, NEG)
             s_ref[c] = s
             m = jnp.max(s, axis=1, keepdims=True)
-            m_ref[...] = jnp.where(lanes == row, jnp.maximum(m_ref[...], m), m_ref[...])
-
-
-def mix_kernel(row_ref, vis_ref, lat_ref, s_ref, m_ref, up_ref, out_ref, l_ref, o_ref):
+            best = jnp.where(lanes == row, jnp.maximum(best, m), best)
+        m_ref[...] = best
+
+
+def mix_kernel(slot_ref, row_ref, vis_ref, *refs):
+    vals = refs[:CHUNK]
+    s_ref, m_ref, out_ref, l_ref, o_ref = refs[CHUNK:]
     step = pl.program_id(0)
 
     @pl.when(step == 0)
@@ -194,25 +204,29 @@
         l_ref[...] = jnp.zeros(l_ref.shape, jnp.float32)
 
     lanes = lax.broadcasted_iota(jnp.int32, (ROWS, BLOCK), 1)
-    flat = lat_ref[...].reshape(CHUNK * BLOCK, R)
-    vals = project(flat, up_ref[...])
-    for c in range(CHUNK):
-        row = row_ref[step * CHUNK + c]
-        vis = vis_ref[step * CHUNK + c]
-
-        @pl.when(vis > 0)
-        def _():
-            m = jnp.max(jnp.where(lanes == row, m_ref[...], NEG), axis=1, keepdims=True)
+
+    @pl.when(vis_ref[step * CHUNK] > 0)
+    def _():
+        best = m_ref[...]
+        sums = l_ref[...]
+        for c in range(CHUNK):
+            row = row_ref[step * CHUNK + c]
+            m = jnp.max(jnp.where(lanes == row, best, NEG), axis=1, keepdims=True)
             p = jnp.exp(s_ref[c] - m)
             total = jnp.sum(p, axis=1, keepdims=True)
-            l_ref[...] = jnp.where(lanes == row, l_ref[...] + total, l_ref[...])
+            sums = jnp.where(lanes == row, sums + total, sums)
             p = p.astype(jnp.bfloat16)
+            parts = []
             for g in range(HK):
-                o_ref[row, g * 32 : (g + 1) * 32, :] += jnp.dot(
-                    p[g * 32 : (g + 1) * 32],
-                    vals[c * BLOCK : (c + 1) * BLOCK, g * HD : (g + 1) * HD],
-                    preferred_element_type=jnp.float32,
+                parts.append(
+                    jnp.dot(
+                        p[g * 32 : (g + 1) * 32],
+                        vals[c][:, g * HD : (g + 1) * HD],
+                        preferred_element_type=jnp.float32,
+                    )
                 )
+            o_ref[row] += jnp.concatenate(parts, axis=0)
+        l_ref[...] = sums
 
     @pl.when(step == pl.num_programs(0) - 1)
     def _():
@@ -252,82 +266,125 @@
     )
 
 
-def gather_kernel(q_ref, up_ref, q_out, up_out, ys, yr, zs, zr, cs, cr, own):
+def gather_kernel(
+    q_ref, up_ref, lat_ref, q_out, up_out, k_out, v_out, ys, yr, zs, zr, cs, cr, own
+):
     z, y, c = coords()
     meet(z, y, c)
     depth = up_ref.shape[1]
-
-    def shard(d):
-        rows = pl.ds(pl.multiple_of(d * depth, depth), depth)
-        return up_out.at[:, rows, :], q_out.at[d]
-
-    def copies(source, d, ssem, rsem, dev):
-        return [
-            send(s, t, ssem.at[n], rsem.at[n], dev)
-            for n, (s, t) in enumerate(zip(source, shard(d)))
-        ]
-
     me = at(z, y, c)
-    mine = (up_ref, q_ref)
-    local_copies = [
-        pltpu.make_async_copy(s, t, own.at[n]) for n, (s, t) in enumerate(zip(mine, shard(me)))
-    ]
     y_dev, c_dev = at(z, 1 - y, c), at(z, y, 1 - c)
-    y_send, z_send, c_send = [], [], []
-    y_send += copies(mine, me, ys.at[0], yr.at[0], y_dev)
-    for k in (1, 2, 3):
-        z_send += copies(mine, me, zs.at[k], zr.at[k], at((z + k) % NZ, y, c))
-    c_send += copies(mine, me, cs.at[0], cr.at[0], c_dev)
-    for cp in y_send + z_send + c_send + local_copies:
+    sends = []
+
+    def shard(n, d):
+        if n == 0:
+            return up_out.at[:, pl.ds(pl.multiple_of(d * depth, depth), depth), :]
+        return q_out.at[d]
+
+    def post(n, source, d, ssem, rsem, k, dev):
+        cp = send(source, shard(n, d), ssem.at[k, n], rsem.at[k, n], dev)
         cp.start()
-
-    def arrived(d, sem):
-        for n, t in enumerate(shard(d)):
-            send(t, t, own.at[n], sem.at[n], y_dev).wait_recv()
-
-    def forward(d, ssem, rsem, dev):
-        more = copies(shard(d), d, ssem, rsem, dev)
-        for cp in more:
-            cp.start()
-        return more
-
-    arrived(at(z, 1 - y, c), yr.at[0])
-    c_send += forward(at(z, 1 - y, c), cs.at[4], cr.at[4], c_dev)
-    for k in (1, 2, 3):
-        d = at((z - k + NZ) % NZ, y, c)
-        arrived(d, zr.at[k])
-        y_send += forward(d, ys.at[k], yr.at[k], y_dev)
-        c_send += forward(d, cs.at[k], cr.at[k], c_dev)
-    for k in (1, 2, 3):
-        d = at((z - k + NZ) % NZ, 1 - y, c)
-        arrived(d, yr.at[k])
-        c_send += forward(d, cs.at[4 + k], cr.at[4 + k], c_dev)
-    for k in range(NZ):
-        for w in range(NY):
-            arrived(at((z - k + NZ) % NZ, (y + w) % NY, 1 - c), cr.at[4 * w + k])
-    for cp in y_send + z_send + c_send:
+        sends.append(cp)
+
+    def arrived(n, d, sem, k):
+        send(shard(n, d), shard(n, d), own.at[n], sem.at[k, n], y_dev).wait_recv()
+
+    def begin(n):
+        mine = (up_ref, q_ref)[n]
+        post(n, mine, me, ys, yr, 0, y_dev)
+        for k in (1, 2, 3):
+            post(n, mine, me, zs, zr, k, at((z + k) % NZ, y, c))
+        post(n, mine, me, cs, cr, 0, c_dev)
+        cp = pltpu.make_async_copy(mine, shard(n, me), own.at[n])
+        cp.start()
+        return cp
+
+    def back(k):
+        return (z - k + NZ) % NZ
+
+    def from_z(n, k):
+        d = at(back(k), y, c)
+        arrived(n, d, zr, k)
+        post(n, shard(n, d), d, ys, yr, k, y_dev)
+        post(n, shard(n, d), d, cs, cr, k, c_dev)
+
+    def from_y(n, k):
+        d = at(back(k), 1 - y, c)
+        arrived(n, d, yr, k)
+        post(n, shard(n, d), d, cs, cr, 4 + k, c_dev)
+
+    def from_c(n):
+        for k in range(NZ):
+            for w in range(NY):
+                arrived(n, at(back(k), (y + w) % NY, 1 - c), cr, 4 * w + k)
+
+    def body(lat, k_blk, v_blk):
+        flat = lat[...].reshape(CHUNK * BLOCK, 2 * R)
+        k_blk[...] = project(flat[:, :R], up_out[0]).reshape(k_blk.shape)
+        v_blk[...] = project(flat[:, R:], up_out[1]).reshape(v_blk.shape)
+
+    def compute(lo, hi):
+        def idx(i):
+            return (i + lo, 0, 0)
+
+        pltpu.emit_pipeline(
+            body,
+            grid=(hi - lo,),
+            in_specs=[pl.BlockSpec((CHUNK, BLOCK, 2 * R), idx)],
+            out_specs=[pl.BlockSpec((CHUNK, BLOCK, HK * HD), idx)] * 2,
+        )(lat_ref, k_out, v_out)
+
+    local_copies = [begin(0)]
+    local_copies.append(begin(1))
+    from_y(0, 0)
+    for k in (1, 3, 2):
+        from_z(0, k)
+    for k in (1, 3, 2):
+        from_y(0, k)
+    from_c(0)
+    local_copies[0].wait()
+    steps = lat_ref.shape[0] // CHUNK
+    cuts = [0, steps // 4, steps // 2, steps * 3 // 4, steps]
+    from_y(1, 0)
+    from_z(1, 1)
+    compute(cuts[0], cuts[1])
+    from_z(1, 3)
+    from_z(1, 2)
+    compute(cuts[1], cuts[2])
+    from_y(1, 1)
+    compute(cuts[2], cuts[3])
+    from_y(1, 3)
+    from_y(1, 2)
+    compute(cuts[3], cuts[4])
+    from_c(1)
+    for cp in sends:
         cp.wait_send()
-    for cp in local_copies:
-        cp.wait()
-
-
-def gather(heads, up_proj):
+    local_copies[1].wait()
+
+
+def gather(heads, up_proj, latents):
     count, rows, width = heads.shape
     two, depth, cols = up_proj.shape
+    slots, block = latents.shape[:2]
     n = NZ * NY * NC
     hbm = pl.BlockSpec(memory_space=pl.ANY)
+    vmem = pl.BlockSpec(memory_space=pltpu.VMEM)
     dma = pltpu.SemaphoreType.DMA
     return pl.pallas_call(
         gather_kernel,
-        in_specs=[hbm, hbm],
-        out_specs=[hbm, hbm],
+        in_specs=[hbm, hbm, hbm],
+        out_specs=[hbm, vmem, hbm, hbm],
         out_shape=[
             jax.ShapeDtypeStruct((n, count, rows, width), heads.dtype),
             jax.ShapeDtypeStruct((two, n * depth, cols), up_proj.dtype),
+            jax.ShapeDtypeStruct((slots, block, cols), up_proj.dtype),
+            jax.ShapeDtypeStruct((slots, block, cols), up_proj.dtype),
         ],
         scratch_shapes=[dma((4, 2))] * 4 + [dma((8, 2))] * 2 + [dma((2,))],
-        compiler_params=pltpu.CompilerParams(collective_id=0, has_side_effects=True),
-    )(heads, up_proj)
+        compiler_params=pltpu.CompilerParams(
+            collective_id=0, has_side_effects=True, vmem_limit_bytes=40 * 2**20
+        ),
+    )(heads, up_proj, latents)
 
 
 def max_kernel(m_ref, out_ref, buf, stage, ss, rs):
@@ -456,6 +513,15 @@
     )(o, l)
 
 
+def picked():
+    def spec(c):
+        return pl.BlockSpec(
+            (None, BLOCK, HK * HD), lambda i, slot, row, vis: (slot[i * CHUNK + c], 0, 0)
+        )
+
+    return [spec(c) for c in range(CHUNK)]
+
+
 def whole(shape):
     return pl.BlockSpec(shape, lambda i, *_: (0,) * len(shape))
 
@@ -469,21 +535,20 @@
             latents, queries, new_latents, up_proj, lengths, place, block_src, block_slot
         )
     device = lax.axis_index("seq")
-    row, vis = slot_plan(lengths, place, block_src, block_slot, device, slot_count)
+    plan = slot_plan(lengths, place, block_src, block_slot, device, slot_count)
     heads = queries.reshape(count, STEPS, HK, GROUP, HD).transpose(0, 2, 1, 3, 4)
     heads = heads.reshape(count, ROWS, HD)
-    q_all, up = gather(heads, up_proj)
+    q_all, up, keys, vals = gather(heads, up_proj, latents)
     q_all = q_all.reshape(requests, ROWS, HD)
     steps = slot_count // CHUNK
     s, m = pl.pallas_call(
         scores_kernel,
         grid_spec=pltpu.PrefetchScalarGridSpec(
-            num_scalar_prefetch=2,
+            num_scalar_prefetch=3,
             grid=(steps,),
             in_specs=[
-                pl.BlockSpec((CHUNK, BLOCK, R), lambda i, *_: (i, 0, 0)),
+                *picked(),
                 whole((requests, ROWS, HD)),
-                pl.BlockSpec((None, R, HK * HD), lambda i, *_: (0, 0, 0)),
             ],
             out_specs=[
                 pl.BlockSpec((CHUNK, ROWS, BLOCK), lambda i, *_: (i, 0, 0)),
@@ -495,7 +560,7 @@
             jax.ShapeDtypeStruct((ROWS, BLOCK), jnp.float32),
         ],
         compiler_params=pltpu.CompilerParams(vmem_limit_bytes=48 * 2**20),
-    )(row, vis, latents, q_all, up)
+    )(*plan, *[keys] * CHUNK, q_all)
     fresh_k = project(new_latents[:, :, :R], up[0]).reshape(count, STEPS, HK, HD)
     fresh_v = project(new_latents[:, :, R:], up[1]).reshape(count, STEPS, HK, HD)
     q_own = heads.reshape(count, HK, STEPS * GROUP, HD)
@@ -513,13 +578,12 @@
     o, l = pl.pallas_call(
         mix_kernel,
         grid_spec=pltpu.PrefetchScalarGridSpec(
-            num_scalar_prefetch=2,
+            num_scalar_prefetch=3,
             grid=(steps,),
             in_specs=[
-                pl.BlockSpec((CHUNK, BLOCK, R), lambda i, *_: (i, 0, 1)),
+                *picked(),
                 pl.BlockSpec((CHUNK, ROWS, BLOCK), lambda i, *_: (i, 0, 0)),
                 whole((ROWS, BLOCK)),
-                pl.BlockSpec((None, R, HK * HD), lambda i, *_: (1, 0, 0)),
             ],
             out_specs=[whole((requests, ROWS, HD)), whole((ROWS, BLOCK))],
             scratch_shapes=[pltpu.VMEM((requests, ROWS, HD), jnp.float32)],
@@ -529,7 +593,7 @@
             jax.ShapeDtypeStruct((ROWS, BLOCK), jnp.float32),
         ],
         compiler_params=pltpu.CompilerParams(vmem_limit_bytes=48 * 2**20),
-    )(row, vis, latents, s, m_cols, up)
+    )(*plan, *[vals] * CHUNK, s, m_cols)
     devices = lax.axis_size("seq")
     o, l = scatter(
         o.reshape(devices, count * ROWS, HD), l[:, :requests].T.reshape(devices, count, ROWS)

time: 158 us -> 149 us (0.943)
  Pallas kernels: 139 us -> 130 us
    pallas_call x1, Pallas kernels: 39 us -> 46.3 us  [gather(): pl.pallas_call(gather_kernel, in_specs=[hbm, hbm, hbm], out_specs=[hbm, v...]
    pallas_call x1, Pallas kernels: 26.6 us -> 20.1 us  [local(): pl.pallas_call(scores_kernel, grid_spec=pltpu.PrefetchScalarGridSpec(num_...]
    pallas_call x1, Pallas kernels: 23.9 us -> 18 us  [local(): pl.pallas_call(mix_kernel, grid_spec=pltpu.PrefetchScalarGridSpec(num_sca...]
    pallas_call x1, Pallas kernels: 19.2 us -> 15.5 us  [global_max(): pl.pallas_call(max_kernel, in_specs=[vmem], out_specs=vmem, out_shape=jax...]
    unnamed x15 -> x13, local copies, waits for them, and re-layouts: 8.05 us -> 7.66 us
where the time goes in v3:
time: 149 us; the launch traced here: 148 us
  Pallas kernels  130 us (87%)
  local copies, waits for them, and re-layouts  11.9 us (8%)
  other arithmetic  3.23 us (2%)
  matrix products  2.96 us (2%)
    pallas_call x1, Pallas kernels, gather(): pl.pallas_call(gather_kernel, in_specs=[hbm, hbm, hbm], out_specs=[hbm, v...  46.3 us
    pallas_call x1, Pallas kernels, scatter(): pl.pallas_call(scatter_kernel, in_specs=[vmem, vmem], out_specs=[vmem, vm...  30 us
    pallas_call x1, Pallas kernels, local(): pl.pallas_call(scores_kernel, grid_spec=pltpu.PrefetchScalarGridSpec(num_...  20.1 us
    pallas_call x1, Pallas kernels, local(): pl.pallas_call(mix_kernel, grid_spec=pltpu.PrefetchScalarGridSpec(num_sca...  18 us
    pallas_call x1, Pallas kernels, global_max(): pl.pallas_call(max_kernel, in_specs=[vmem], out_specs=vmem, out_shape=jax...  15.5 us
    unnamed x13, local copies, waits for them, and re-layouts  7.66 us

profile of v3, /device:TPU:0, one launch (start us, length us, event | category | flops | bytes accessed | tf_op | source)
XLA Modules:
  0.0 148.1 jit_solution(3031696022547620542)
XLA Ops:
  0.0 0.7 broadcast_multiply_fusion
  0.7 0.7 broadcast_compare_fusion
  1.5 0.7 clamp_add_fusion
  2.2 0.8 copy.27
  3.0 0.7 select_reduce_fusion
  3.8 0.2 convert_reduce_fusion
  3.9 0.1 select_reduce_fusion.1
  4.1 1.1 reshape.149
  5.3 3.7 %copy-done = bf16[72,128,512]{2,1,0:T(8,128)(2,1)S(1)} copy-done((bf16[72,128,512]{2,1,0:T(8,128)(2,1)S(1)}, bf16[72,128,512]{2,1,0:T(8,128)(2,1)}, u32[]{:S(2)}) %copy-start) | copy-done | bytes 9437208
  9.0 0.8 copy-done.1
  9.8 46.3 %shard_map.82 = (bf16[16,3,256,128]{3,2,1,0:T(8,128)(2,1)S(1)}, bf16[2,256,1024]{2,1,0:T(8,128)(2,1)S(1)}, bf16[72,128,1024]{2,1,0:T(8,128)(2,1)}, bf16[72,128,1024]{2,1,0:T(8,128)(2,1)}) custom-call(bf16[3,256,128]{2,1,0:T(8,128)(2,1)S(1)} %bitcast.57, bf16[2,16,1024]{2,1,0:T(8,128)(2,1)S(1)} %copy-done.1, bf16[72,128,512]{2,1,0:T(8,128)(2,1)S(1)} %copy-done), custom_call_target="tpu_custom_call" | custom-call | tf_op jit(solution)/shard_map/pallas_call | solution.py:373
  56.1 1.0 copy-done.2
  57.1 1.4 fusion.34
  58.6 20.1 %shard_map.83 = (f32[72,256,128]{2,1,0:T(8,128)}, f32[256,128]{1,0:T(8,128)S(1)}) custom-call(s32[72]{0:T(128)S(1)} %get-tuple-element.31.slot_ref, s32[72]{0:T(128)S(1)} %get-tuple-element.30.row_ref, s32[72]{0:T(128)S(1)} %get-tuple-element.29.vis_ref, bf16[72,128,1024]{2,1,0:T(8,128)(2,1)} %get-tuple-element.16.refs_0_.refs_1_.refs_2_.refs_3_, ...), custom_call_target="tpu_custom_call" | custom-call | tf_op jit(solution)/shard_map/pallas_call | solution.py:544
  78.9 0.2 dynamic_update_slice.3.m_ref
  79.1 0.6 copy-done.4
  79.7 15.5 %shard_map.84 = f32[48,256]{1,0:T(8,128)} custom-call(f32[48,256]{1,0:T(8,128)} %copy-done.4), custom_call_target="tpu_custom_call" | custom-call | tf_op jit(solution)/shard_map/pallas_call | solution.py:413
  95.1 0.7 constant_dynamic-slice_fusion
  96.0 0.9 copy.32
  96.9 18.0 %shard_map.85 = (bf16[48,256,128]{2,1,0:T(8,128)(2,1)S(1)}, f32[256,128]{1,0:T(8,128)S(1)}) custom-call(s32[72]{0:T(128)S(1)} %get-tuple-element.31.slot_ref, s32[72]{0:T(128)S(1)} %get-tuple-element.30.row_ref, s32[72]{0:T(128)S(1)} %get-tuple-element.29.vis_ref, bf16[72,128,1024]{2,1,0:T(8,128)(2,1)} %get-tuple-element.15.refs_0_.refs_1_.refs_2_.refs_3_, ...), custom_call_target="tpu_custom_call" | custom-call | tf_op jit(solution)/shard_map/pallas_call | solution.py:578
  115.0 30.0 %shard_map.86 = (f32[768,128]{1,0:T(8,128)S(1)}, f32[3,256]{1,0:T(4,128)S(1)}) custom-call(bf16[16,768,128]{2,1,0:T(8,128)(2,1)S(1)} %bitcast.56, f32[16,3,256]{2,1,0:T(4,128)S(1)} %reshape.155.l_ref), custom_call_target="tpu_custom_call" | custom-call | tf_op jit(solution)/shard_map/pallas_call | solution.py:500
  145.0 0.7 copy-done.3
  145.8 1.5 %fusion.2 = bf16[3,4,8,8,128]{4,3,1,2,0:T(8,128)(2,1)S(1)} fusion(f32[3,8,32,128]{3,2,1,0:T(8,128)} %bitcast.58, bf16[2,256,1024]{2,1,0:T(8,128)(2,1)} %copy-done.2, f32[3,8,32]{2,1,0:T(8,128)S(1)} %add.76, f32[3,8,32,4]{2,3,1,0:T(4,128)S(1)} %get-tuple-element.33, f32[3,8,32]{2,1,0:T(8,128)S(1)} %sub.49, bf16[3,4,512]{2,1,0:T(4,128)(2,1)S(1)} %copy-done.5), kind=kOutput, calls=%fused_computation.3 | convolution fusion | flops 7391232 | bytes 1193984 | tf_op jit(solution)/shard_map/bgrt,btgd->bgrd/dot_general | solution.py:603
  147.4 0.7 reshape.160
  (28 shorter events, 0.8 us)
Async XLA Ops:
  0.0 57.1 %copy-start.5 = (bf16[3,4,512]{2,1,0:T(4,128)(2,1)S(1)}, bf16[3,4,512]{2,1,0:T(4,128)(2,1)}, u32[]{:S(2)}) copy-start(bf16[3,4,512]{2,1,0:T(4,128)(2,1)} %param.10) | copy-start | bytes 36868
  5.3 3.7 %copy-start = (bf16[72,128,512]{2,1,0:T(8,128)(2,1)S(1)}, bf16[72,128,512]{2,1,0:T(8,128)(2,1)}, u32[]{:S(2)}) copy-start(bf16[72,128,512]{2,1,0:T(8,128)(2,1)} %lat_ref.1) | copy-start | bytes 28311556
  9.0 0.8 copy-start.1
  56.1 1.0 copy-start.2
  79.1 0.6 copy-start.4
  145.0 0.7 copy-start.3

commit v4 on v3

--- a/solution.py
+++ b/solution.py
@@ -266,8 +266,21 @@
     )
 
 
+def project_slots(lo, hi, lat_ref, up_ref, out_ref, part):
+    def body(lat, out):
+        flat = lat[...].reshape(CHUNK * BLOCK, R)
+        out[...] = project(flat, up_ref[...]).reshape(out.shape)
+
+    pltpu.emit_pipeline(
+        body,
+        grid=(hi - lo,),
+        in_specs=[pl.BlockSpec((CHUNK, BLOCK, R), lambda i: (i + lo, 0, part))],
+        out_specs=[pl.BlockSpec((CHUNK, BLOCK, HK * HD), lambda i: (i + lo, 0, 0))],
+    )(lat_ref, out_ref)
+
+
 def gather_kernel(
-    q_ref, up_ref, lat_ref, q_out, up_out, k_out, v_out, ys, yr, zs, zr, cs, cr, own
+    q_ref, up_ref, lat_ref, q_out, up_out, k_out, ys, yr, zs, zr, cs, cr, own
 ):
     z, y, c = coords()
     meet(z, y, c)
@@ -318,21 +331,8 @@
             for w in range(NY):
                 arrived(n, at(back(k), (y + w) % NY, 1 - c), cr, 4 * w + k)
 
-    def body(lat, k_blk, v_blk):
-        flat = lat[...].reshape(CHUNK * BLOCK, 2 * R)
-        k_blk[...] = project(flat[:, :R], up_out[0]).reshape(k_blk.shape)
-        v_blk[...] = project(flat[:, R:], up_out[1]).reshape(v_blk.shape)
-
     def compute(lo, hi):
-        def idx(i):
-            return (i + lo, 0, 0)
-
-        pltpu.emit_pipeline(
-            body,
-            grid=(hi - lo,),
-            in_specs=[pl.BlockSpec((CHUNK, BLOCK, 2 * R), idx)],
-            out_specs=[pl.BlockSpec((CHUNK, BLOCK, HK * HD), idx)] * 2,
-        )(lat_ref, k_out, v_out)
+        project_slots(lo, hi, lat_ref, up_out.at[0], k_out, 0)
 
     local_copies = [begin(0)]
     local_copies.append(begin(1))
@@ -373,27 +373,29 @@
     return pl.pallas_call(
         gather_kernel,
         in_specs=[hbm, hbm, hbm],
-        out_specs=[hbm, vmem, hbm, hbm],
+        out_specs=[hbm, vmem, hbm],
         out_shape=[
             jax.ShapeDtypeStruct((n, count, rows, width), heads.dtype),
             jax.ShapeDtypeStruct((two, n * depth, cols), up_proj.dtype),
             jax.ShapeDtypeStruct((slots, block, cols), up_proj.dtype),
-            jax.ShapeDtypeStruct((slots, block, cols), up_proj.dtype),
         ],
         scratch_shapes=[dma((4, 2))] * 4 + [dma((8, 2))] * 2 + [dma((2,))],
         compiler_params=pltpu.CompilerParams(
-            collective_id=0, has_side_effects=True, vmem_limit_bytes=40 * 2**20
+            collective_id=0, has_side_effects=True, vmem_limit_bytes=60 * 2**20
         ),
     )(heads, up_proj, latents)
 
 
-def max_kernel(m_ref, out_ref, buf, stage, ss, rs):
+def max_kernel(m_ref, up_ref, lat_ref, out_ref, v_out, buf, stage, ss, rs):
     z, y, c = coords()
+    steps = lat_ref.shape[0] // CHUNK
+    cuts = [0, steps // 4, steps // 2, steps]
     meet(z, y, c)
     stage[0] = m_ref[...]
     for n, dev in ((0, at(z, y, 1 - c)), (1, at(z, 1 - y, c))):
         cp = send(stage.at[n], buf.at[n], ss.at[n], rs.at[n], dev)
         cp.start()
+        project_slots(cuts[n], cuts[n + 1], lat_ref, up_ref.at[1], v_out, 1)
         cp.wait()
         stage[n + 1] = jnp.maximum(stage[n], buf[n])
     cps = [
@@ -402,88 +404,106 @@
     ]
     for cp in cps:
         cp.start()
+    project_slots(cuts[2], cuts[3], lat_ref, up_ref.at[1], v_out, 1)
     for cp in cps:
         cp.wait()
     out_ref[...] = jnp.maximum(jnp.maximum(stage[2], buf[2]), jnp.maximum(buf[3], buf[4]))
 
 
-def global_max(m):
+def global_max(m, up, latents):
+    slots, block = latents.shape[:2]
+    hbm = pl.BlockSpec(memory_space=pl.ANY)
     vmem = pl.BlockSpec(memory_space=pltpu.VMEM)
     dma = pltpu.SemaphoreType.DMA
     return pl.pallas_call(
         max_kernel,
-        in_specs=[vmem],
-        out_specs=vmem,
-        out_shape=jax.ShapeDtypeStruct(m.shape, m.dtype),
+        in_specs=[vmem, vmem, hbm],
+        out_specs=[vmem, hbm],
+        out_shape=[
+            jax.ShapeDtypeStruct(m.shape, m.dtype),
+            jax.ShapeDtypeStruct((slots, block, up.shape[2]), up.dtype),
+        ],
         scratch_shapes=[
             pltpu.VMEM((5,) + m.shape, m.dtype),
             pltpu.VMEM((3,) + m.shape, m.dtype),
             dma((5,)),
             dma((5,)),
         ],
-        compiler_params=pltpu.CompilerParams(collective_id=1, has_side_effects=True),
-    )(m)
-
-
-def scatter_kernel(o_ref, l_ref, o_out, l_out, cb, cl, yb, yl, yi, yj, zb, zl, zi, zj, cs, cr, ys, yr, zs, zr):
+        compiler_params=pltpu.CompilerParams(
+            collective_id=1, has_side_effects=True, vmem_limit_bytes=60 * 2**20
+        ),
+    )(m, up, latents)
+
+
+def scatter_kernel(
+    o_ref, l_ref, o_out, l_out, cb, cl, yb, yl, yi, yj, zb, zl, zi, zj, cs, cr, ys, yr, zs, zr
+):
     z, y, c = coords()
     meet(z, y, c)
     y_dev, c_dev = at(z, 1 - y, c), at(z, y, 1 - c)
     order = [(z + 1) % NZ, (z + 2) % NZ, (z + 3) % NZ, z]
+    half = o_ref.shape[1] // 2
+    f32 = jnp.float32
     sends = []
 
-    def pair(so, sl, to, tl, ssem, rsem, dev):
-        cps = [
-            send(so, to, ssem.at[0], rsem.at[0], dev),
-            send(sl, tl, ssem.at[1], rsem.at[1], dev),
-        ]
+    def rows(h):
+        return slice(h * half, (h + 1) * half)
+
+    def piece(h, so, sl, to, tl, ssem, rsem, dev):
+        part = pl.ds(h * half, half)
+        cps = [send(so.at[part], to.at[part], ssem.at[h], rsem.at[h], dev)]
+        if h == 0:
+            cps.append(send(sl, tl, ssem.at[2], rsem.at[2], dev))
         for cp in cps:
             cp.start()
         sends.extend(cps)
         return cps
 
-    c_in = {}
+    pieces = [(k, h) for k in range(NZ) for h in (0, 1)]
+    c_in, y_in, z_in = {}, {}, {}
     for w in (1, 0):
-        for k in range(NZ):
+        for k, h in pieces:
             d = at(order[k], (y + w) % NY, 1 - c)
             i = 4 * w + k
-            c_in[w, k] = pair(
-                o_ref.at[d], l_ref.at[d], cb.at[i], cl.at[i], cs.at[i], cr.at[i], c_dev
+            c_in[w, k, h] = piece(
+                h, o_ref.at[d], l_ref.at[d], cb.at[i], cl.at[i], cs.at[i], cr.at[i], c_dev
             )
-    f32 = jnp.float32
-    y_in = []
-    for k in range(NZ):
-        for cp in c_in[1, k]:
+    for k, h in pieces:
+        for cp in c_in[1, k, h]:
             cp.wait_recv()
         d = at(order[k], 1 - y, c)
-        yb[k] = (o_ref[d].astype(f32) + cb[4 + k].astype(f32)).astype(jnp.bfloat16)
-        yl[k] = l_ref[d] + cl[4 + k]
-        y_in.append(
-            pair(yb.at[k], yl.at[k], yi.at[k], yj.at[k], ys.at[k], yr.at[k], y_dev)
-        )
-    z_in = []
-    for k in range(NZ):
-        for cp in c_in[0, k] + y_in[k]:
+        yb[k, rows(h)] = (
+            o_ref[d, rows(h)].astype(f32) + cb[4 + k, rows(h)].astype(f32)
+        ).astype(jnp.bfloat16)
+        if h == 0:
+            yl[k] = l_ref[d] + cl[4 + k]
+        y_in[k, h] = piece(h, yb.at[k], yl.at[k], yi.at[k], yj.at[k], ys.at[k], yr.at[k], y_dev)
+    for k, h in pieces:
+        for cp in c_in[0, k, h] + y_in[k, h]:
             cp.wait_recv()
         d = at(order[k], y, c)
-        o = o_ref[d].astype(f32) + cb[k].astype(f32) + yi[k].astype(f32)
-        l = l_ref[d] + cl[k] + yj[k]
+        o = (
+            o_ref[d, rows(h)].astype(f32)
+            + cb[k, rows(h)].astype(f32)
+            + yi[k, rows(h)].astype(f32)
+        )
         if k < NZ - 1:
-            zb[k] = o.astype(jnp.bfloat16)
-            zl[k] = l
-            z_in.append(
-                pair(
-                    zb.at[k], zl.at[k], zi.at[k], zj.at[k], zs.at[k], zr.at[k], at(order[k], y, c)
-                )
+            zb[k, rows(h)] = o.astype(jnp.bfloat16)
+            if h == 0:
+                zl[k] = l_ref[d] + cl[k] + yj[k]
+            z_in[k, h] = piece(
+                h, zb.at[k], zl.at[k], zi.at[k], zj.at[k], zs.at[k], zr.at[k], at(order[k], y, c)
             )
         else:
-            o_out[...] = o
-            l_out[...] = l
-    for k in range(NZ - 1):
-        for cp in z_in[k]:
+            o_out[rows(h)] = o
+            if h == 0:
+                l_out[...] = l_ref[d] + cl[k] + yj[k]
+    for k, h in pieces[: 2 * (NZ - 1)]:
+        for cp in z_in[k, h]:
             cp.wait_recv()
-        o_out[...] += zi[k].astype(f32)
-        l_out[...] += zj[k]
+        o_out[rows(h)] += zi[k, rows(h)].astype(f32)
+        if h == 0:
+            l_out[...] += zj[k]
     for cp in sends:
         cp.wait_send()
 
@@ -506,7 +526,7 @@
             jax.ShapeDtypeStruct((lr, lw), jnp.float32),
         ],
         scratch_shapes=bufs(8) + bufs(4) + bufs(4) + bufs(3) + bufs(3)
-        + [dma((8, 2))] * 2 + [dma((4, 2))] * 2 + [dma((3, 2))] * 2,
+        + [dma((8, 3))] * 2 + [dma((4, 3))] * 2 + [dma((3, 3))] * 2,
         compiler_params=pltpu.CompilerParams(
             collective_id=2, has_side_effects=True, vmem_limit_bytes=40 * 2**20
         ),
@@ -538,7 +558,7 @@
     plan = slot_plan(lengths, place, block_src, block_slot, device, slot_count)
     heads = queries.reshape(count, STEPS, HK, GROUP, HD).transpose(0, 2, 1, 3, 4)
     heads = heads.reshape(count, ROWS, HD)
-    q_all, up, keys, vals = gather(heads, up_proj, latents)
+    q_all, up, keys = gather(heads, up_proj, latents)
     q_all = q_all.reshape(requests, ROWS, HD)
     steps = slot_count // CHUNK
     s, m = pl.pallas_call(
@@ -572,7 +592,7 @@
     m = m[:, :requests].T
     own = lax.dynamic_slice(m, (first, 0), (count, ROWS))
     m = lax.dynamic_update_slice(m, jnp.maximum(own, fm), (first, 0))
-    m = global_max(m)
+    m, vals = global_max(m, up, latents)
     own = lax.dynamic_slice(m, (first, 0), (count, ROWS)).reshape(count, HK, STEPS * GROUP)
     m_cols = jnp.pad(m.T, ((0, 0), (0, BLOCK - requests)))
     o, l = pl.pallas_call(

time: 149 us -> 154 us (1.034)
  Pallas kernels: 130 us -> 137 us
  local copies, waits for them, and re-layouts: 11.9 us -> 8.98 us
    pallas_call x1, Pallas kernels: 15.5 us -> 25.7 us  [global_max(): pl.pallas_call(max_kernel, in_specs=[vmem, vmem, hbm], out_specs=[vmem, h...]
    unnamed x13 -> x9, local copies, waits for them, and re-layouts: 7.66 us -> 4.02 us
    pallas_call x1, Pallas kernels: 30 us -> 27.1 us  [scatter(): pl.pallas_call(scatter_kernel, in_specs=[vmem, vmem], out_specs=[vmem, vm...]
where the time goes in v4:
time: 154 us; the launch traced here: 153 us
  Pallas kernels  137 us (89%)
  local copies, waits for them, and re-layouts  8.98 us (6%)
  other arithmetic  3.23 us (2%)
  matrix products  2.96 us (2%)
    pallas_call x1, Pallas kernels, gather(): pl.pallas_call(gather_kernel, in_specs=[hbm, hbm, hbm], out_specs=[hbm, v...  45.3 us
    pallas_call x1, Pallas kernels, scatter(): pl.pallas_call(scatter_kernel, in_specs=[vmem, vmem], out_specs=[vmem, vm...  27.1 us
    pallas_call x1, Pallas kernels, global_max(): pl.pallas_call(max_kernel, in_specs=[vmem, vmem, hbm], out_specs=[vmem, h...  25.7 us
    pallas_call x1, Pallas kernels, local(): pl.pallas_call(scores_kernel, grid_spec=pltpu.PrefetchScalarGridSpec(num_...  20.7 us
    pallas_call x1, Pallas kernels, local(): pl.pallas_call(mix_kernel, grid_spec=pltpu.PrefetchScalarGridSpec(num_sca...  18.4 us
    unnamed x9, local copies, waits for them, and re-layouts  4.02 us

profile of v4, /device:TPU:0, one launch (start us, length us, event | category | flops | bytes accessed | tf_op | source)
XLA Modules:
  0.0 152.6 jit_solution(2173788500384318081)
XLA Ops:
  0.0 0.7 broadcast_multiply_fusion
  0.7 0.7 broadcast_compare_fusion
  1.4 0.1 copy.28
  1.5 0.7 clamp_add_fusion
  2.2 0.8 copy.27
  3.0 0.7 select_reduce_fusion
  3.8 0.2 convert_reduce_fusion
  3.9 0.1 select_reduce_fusion.1
  4.1 1.1 reshape.149
  5.2 0.7 copy.29
  5.9 45.3 %shard_map.82 = (bf16[16,3,256,128]{3,2,1,0:T(8,128)(2,1)}, bf16[2,256,1024]{2,1,0:T(8,128)(2,1)}, bf16[72,128,1024]{2,1,0:T(8,128)(2,1)}) custom-call(bf16[3,256,128]{2,1,0:T(8,128)(2,1)} %bitcast.58, bf16[2,16,1024]{2,1,0:T(8,128)(2,1)} %up_ref.1, bf16[72,128,512]{2,1,0:T(8,128)(2,1)} %lat_ref.3), custom_call_target="tpu_custom_call" | custom-call | tf_op jit(solution)/shard_map/pallas_call | solution.py:373
  51.3 1.4 fusion.34
  52.8 1.9 %copy-done = bf16[16,3,256,128]{3,2,1,0:T(8,128)(2,1)S(1)} copy-done((bf16[16,3,256,128]{3,2,1,0:T(8,128)(2,1)S(1)}, bf16[16,3,256,128]{3,2,1,0:T(8,128)(2,1)}, u32[]{:S(2)}) %copy-start) | copy-done | bytes 3145752
  54.7 20.7 %shard_map.83 = (f32[72,256,128]{2,1,0:T(8,128)}, f32[256,128]{1,0:T(8,128)S(1)}) custom-call(s32[72]{0:T(128)S(1)} %get-tuple-element.33.slot_ref, s32[72]{0:T(128)S(1)} %get-tuple-element.32.row_ref, s32[72]{0:T(128)S(1)} %get-tuple-element.31.vis_ref, bf16[72,128,1024]{2,1,0:T(8,128)(2,1)} %get-tuple-element.16.refs_0_.refs_1_.refs_2_.refs_3_, ...), custom_call_target="tpu_custom_call" | custom-call | tf_op jit(solution)/shard_map/pallas_call | solution.py:564
  75.5 0.2 dynamic_update_slice.3.m_ref
  75.7 0.6 copy-done.2
  76.3 25.7 %shard_map.84 = (f32[48,256]{1,0:T(8,128)}, bf16[72,128,1024]{2,1,0:T(8,128)(2,1)}) custom-call(f32[48,256]{1,0:T(8,128)} %copy-done.2, bf16[2,256,1024]{2,1,0:T(8,128)(2,1)} %get-tuple-element.19.up_ref, bf16[72,128,512]{2,1,0:T(8,128)(2,1)} %lat_ref.3), custom_call_target="tpu_custom_call" | custom-call | tf_op jit(solution)/shard_map/pallas_call | solution.py:418
  102.0 0.7 constant_dynamic-slice_fusion
  102.8 0.9 copy.32
  103.8 18.4 %shard_map.85 = (bf16[48,256,128]{2,1,0:T(8,128)(2,1)S(1)}, f32[256,128]{1,0:T(8,128)S(1)}) custom-call(s32[72]{0:T(128)S(1)} %get-tuple-element.33.slot_ref, s32[72]{0:T(128)S(1)} %get-tuple-element.32.row_ref, s32[72]{0:T(128)S(1)} %get-tuple-element.31.vis_ref, bf16[72,128,1024]{2,1,0:T(8,128)(2,1)} %get-tuple-element.20.refs_0_.refs_1_.refs_2_.refs_3_, ...), custom_call_target="tpu_custom_call" | custom-call | tf_op jit(solution)/shard_map/pallas_call | solution.py:598
  122.3 27.1 %shard_map.86 = (f32[768,128]{1,0:T(8,128)S(1)}, f32[3,256]{1,0:T(4,128)S(1)}) custom-call(bf16[16,768,128]{2,1,0:T(8,128)(2,1)S(1)} %bitcast.56, f32[16,3,256]{2,1,0:T(4,128)S(1)} %reshape.155.l_ref), custom_call_target="tpu_custom_call" | custom-call | tf_op jit(solution)/shard_map/pallas_call | solution.py:520
  149.5 0.7 copy-done.1
  150.3 1.5 %fusion.2 = bf16[3,4,8,8,128]{4,3,1,2,0:T(8,128)(2,1)S(1)} fusion(f32[3,8,32,128]{3,2,1,0:T(8,128)} %bitcast.57, bf16[2,256,1024]{2,1,0:T(8,128)(2,1)} %get-tuple-element.19.up_ref, f32[3,8,32]{2,1,0:T(8,128)S(1)} %add.76, f32[3,8,32,4]{2,3,1,0:T(4,128)S(1)} %get-tuple-element.35, f32[3,8,32]{2,1,0:T(8,128)S(1)} %sub.49, bf16[3,4,512]{2,1,0:T(4,128)(2,1)S(1)} %copy-done.3), kind=kOutput, calls=%fused_computation.3 | convolution fusion | flops 7391232 | bytes 1193984 | tf_op jit(solution)/shard_map/bgrt,btgd->bgrd/dot_general | solution.py:623
  151.9 0.7 reshape.160
  (24 shorter events, 0.6 us)
Async XLA Ops:
  0.0 51.3 %copy-start.3 = (bf16[3,4,512]{2,1,0:T(4,128)(2,1)S(1)}, bf16[3,4,512]{2,1,0:T(4,128)(2,1)}, u32[]{:S(2)}) copy-start(bf16[3,4,512]{2,1,0:T(4,128)(2,1)} %param.10) | copy-start | bytes 36868
  52.8 1.9 %copy-start = (bf16[16,3,256,128]{3,2,1,0:T(8,128)(2,1)S(1)}, bf16[16,3,256,128]{3,2,1,0:T(8,128)(2,1)}, u32[]{:S(2)}) copy-start(bf16[16,3,256,128]{3,2,1,0:T(8,128)(2,1)} %get-tuple-element.17) | copy-start | bytes 9437188
  75.7 0.6 copy-start.2
  149.4 0.7 copy-start.1

commit v5 on v4

--- a/solution.py
+++ b/solution.py
@@ -266,21 +266,8 @@
     )
 
 
-def project_slots(lo, hi, lat_ref, up_ref, out_ref, part):
-    def body(lat, out):
-        flat = lat[...].reshape(CHUNK * BLOCK, R)
-        out[...] = project(flat, up_ref[...]).reshape(out.shape)
-
-    pltpu.emit_pipeline(
-        body,
-        grid=(hi - lo,),
-        in_specs=[pl.BlockSpec((CHUNK, BLOCK, R), lambda i: (i + lo, 0, part))],
-        out_specs=[pl.BlockSpec((CHUNK, BLOCK, HK * HD), lambda i: (i + lo, 0, 0))],
-    )(lat_ref, out_ref)
-
-
 def gather_kernel(
-    q_ref, up_ref, lat_ref, q_out, up_out, k_out, ys, yr, zs, zr, cs, cr, own
+    q_ref, up_ref, lat_ref, q_out, up_out, k_out, v_out, ys, yr, zs, zr, cs, cr, own
 ):
     z, y, c = coords()
     meet(z, y, c)
@@ -331,8 +318,21 @@
             for w in range(NY):
                 arrived(n, at(back(k), (y + w) % NY, 1 - c), cr, 4 * w + k)
 
+    def body(lat, k_blk, v_blk):
+        flat = lat[...].reshape(CHUNK * BLOCK, 2 * R)
+        k_blk[...] = project(flat[:, :R], up_out[0]).reshape(k_blk.shape)
+        v_blk[...] = project(flat[:, R:], up_out[1]).reshape(v_blk.shape)
+
     def compute(lo, hi):
-        project_slots(lo, hi, lat_ref, up_out.at[0], k_out, 0)
+        def idx(i):
+            return (i + lo, 0, 0)
+
+        pltpu.emit_pipeline(
+            body,
+            grid=(hi - lo,),
+            in_specs=[pl.BlockSpec((CHUNK, BLOCK, 2 * R), idx)],
+            out_specs=[pl.BlockSpec((CHUNK, BLOCK, HK * HD), idx)] * 2,
+        )(lat_ref, k_out, v_out)
 
     local_copies = [begin(0)]
     local_copies.append(begin(1))
@@ -373,10 +373,11 @@
     return pl.pallas_call(
         gather_kernel,
         in_specs=[hbm, hbm, hbm],
-        out_specs=[hbm, vmem, hbm],
+        out_specs=[hbm, vmem, hbm, hbm],
         out_shape=[
             jax.ShapeDtypeStruct((n, count, rows, width), heads.dtype),
             jax.ShapeDtypeStruct((two, n * depth, cols), up_proj.dtype),
+            jax.ShapeDtypeStruct((slots, block, cols), up_proj.dtype),
             jax.ShapeDtypeStruct((slots, block, cols), up_proj.dtype),
         ],
         scratch_shapes=[dma((4, 2))] * 4 + [dma((8, 2))] * 2 + [dma((2,))],
@@ -386,16 +387,13 @@
     )(heads, up_proj, latents)
 
 
-def max_kernel(m_ref, up_ref, lat_ref, out_ref, v_out, buf, stage, ss, rs):
+def max_kernel(m_ref, out_ref, buf, stage, ss, rs):
     z, y, c = coords()
-    steps = lat_ref.shape[0] // CHUNK
-    cuts = [0, steps // 4, steps // 2, steps]
     meet(z, y, c)
     stage[0] = m_ref[...]
     for n, dev in ((0, at(z, y, 1 - c)), (1, at(z, 1 - y, c))):
         cp = send(stage.at[n], buf.at[n], ss.at[n], rs.at[n], dev)
         cp.start()
-        project_slots(cuts[n], cuts[n + 1], lat_ref, up_ref.at[1], v_out, 1)
         cp.wait()
         stage[n + 1] = jnp.maximum(stage[n], buf[n])
     cps = [
@@ -404,35 +402,27 @@
     ]
     for cp in cps:
         cp.start()
-    project_slots(cuts[2], cuts[3], lat_ref, up_ref.at[1], v_out, 1)
     for cp in cps:
         cp.wait()
     out_ref[...] = jnp.maximum(jnp.maximum(stage[2], buf[2]), jnp.maximum(buf[3], buf[4]))
 
 
-def global_max(m, up, latents):
-    slots, block = latents.shape[:2]
-    hbm = pl.BlockSpec(memory_space=pl.ANY)
+def global_max(m):
     vmem = pl.BlockSpec(memory_space=pltpu.VMEM)
     dma = pltpu.SemaphoreType.DMA
     return pl.pallas_call(
         max_kernel,
-        in_specs=[vmem, vmem, hbm],
-        out_specs=[vmem, hbm],
-        out_shape=[
-            jax.ShapeDtypeStruct(m.shape, m.dtype),
-            jax.ShapeDtypeStruct((slots, block, up.shape[2]), up.dtype),
-        ],
+        in_specs=[vmem],
+        out_specs=vmem,
+        out_shape=jax.ShapeDtypeStruct(m.shape, m.dtype),
         scratch_shapes=[
             pltpu.VMEM((5,) + m.shape, m.dtype),
             pltpu.VMEM((3,) + m.shape, m.dtype),
             dma((5,)),
             dma((5,)),
         ],
-        compiler_params=pltpu.CompilerParams(
-            collective_id=1, has_side_effects=True, vmem_limit_bytes=60 * 2**20
-        ),
-    )(m, up, latents)
+        compiler_params=pltpu.CompilerParams(collective_id=1, has_side_effects=True),
+    )(m)
 
 
 def scatter_kernel(
@@ -558,7 +548,7 @@
     plan = slot_plan(lengths, place, block_src, block_slot, device, slot_count)
     heads = queries.reshape(count, STEPS, HK, GROUP, HD).transpose(0, 2, 1, 3, 4)
     heads = heads.reshape(count, ROWS, HD)
-    q_all, up, keys = gather(heads, up_proj, latents)
+    q_all, up, keys, vals = gather(heads, up_proj, latents)
     q_all = q_all.reshape(requests, ROWS, HD)
     steps = slot_count // CHUNK
     s, m = pl.pallas_call(
@@ -592,7 +582,7 @@
     m = m[:, :requests].T
     own = lax.dynamic_slice(m, (first, 0), (count, ROWS))
     m = lax.dynamic_update_slice(m, jnp.maximum(own, fm), (first, 0))
-    m, vals = global_max(m, up, latents)
+    m = global_max(m)
     own = lax.dynamic_slice(m, (first, 0), (count, ROWS)).reshape(count, HK, STEPS * GROUP)
     m_cols = jnp.pad(m.T, ((0, 0), (0, BLOCK - requests)))
     o, l = pl.pallas_call(

time: 154 us -> 151 us (0.981)
  Pallas kernels: 137 us -> 134 us
    pallas_call x1, Pallas kernels: 25.7 us -> 15.4 us  [global_max(): pl.pallas_call(max_kernel, in_specs=[vmem], out_specs=vmem, out_shape=jax...]
    pallas_call x1, Pallas kernels: 45.3 us -> 52.5 us  [gather(): pl.pallas_call(gather_kernel, in_specs=[hbm, hbm, hbm], out_specs=[hbm, v...]
where the time goes in v5:
time: 151 us; the launch traced here: 149 us
  Pallas kernels  134 us (89%)
  local copies, waits for them, and re-layouts  8.98 us (6%)
  other arithmetic  3.23 us (2%)
  matrix products  2.96 us (2%)
    pallas_call x1, Pallas kernels, gather(): pl.pallas_call(gather_kernel, in_specs=[hbm, hbm, hbm], out_specs=[hbm, v...  52.5 us
    pallas_call x1, Pallas kernels, scatter(): pl.pallas_call(scatter_kernel, in_specs=[vmem, vmem], out_specs=[vmem, vm...  26.8 us
    pallas_call x1, Pallas kernels, local(): pl.pallas_call(scores_kernel, grid_spec=pltpu.PrefetchScalarGridSpec(num_...  20.6 us
    pallas_call x1, Pallas kernels, local(): pl.pallas_call(mix_kernel, grid_spec=pltpu.PrefetchScalarGridSpec(num_sca...  18.4 us
    pallas_call x1, Pallas kernels, global_max(): pl.pallas_call(max_kernel, in_specs=[vmem], out_specs=vmem, out_shape=jax...  15.4 us
    unnamed x9, local copies, waits for them, and re-layouts  4.02 us

profile of v5, /device:TPU:0, one launch (start us, length us, event | category | flops | bytes accessed | tf_op | source)
XLA Modules:
  0.0 149.2 jit_solution(18373550573686652288)
XLA Ops:
  0.0 0.7 broadcast_multiply_fusion
  0.7 0.7 broadcast_compare_fusion
  1.4 0.1 copy.28
  1.5 0.7 clamp_add_fusion
  2.2 0.8 copy.27
  3.0 0.7 select_reduce_fusion
  3.8 0.2 convert_reduce_fusion
  3.9 0.1 select_reduce_fusion.1
  4.1 1.1 reshape.149
  5.2 0.7 copy.29
  5.9 52.5 %shard_map.82 = (bf16[16,3,256,128]{3,2,1,0:T(8,128)(2,1)}, bf16[2,256,1024]{2,1,0:T(8,128)(2,1)}, bf16[72,128,1024]{2,1,0:T(8,128)(2,1)}, bf16[72,128,1024]{2,1,0:T(8,128)(2,1)}) custom-call(bf16[3,256,128]{2,1,0:T(8,128)(2,1)} %bitcast.58, bf16[2,16,1024]{2,1,0:T(8,128)(2,1)} %up_ref.1, bf16[72,128,512]{2,1,0:T(8,128)(2,1)} %lat_ref.1), custom_call_target="tpu_custom_call" | custom-call | tf_op jit(solution)/shard_map/pallas_call | solution.py:373
  58.4 1.4 fusion.34
  60.0 1.9 %copy-done = bf16[16,3,256,128]{3,2,1,0:T(8,128)(2,1)S(1)} copy-done((bf16[16,3,256,128]{3,2,1,0:T(8,128)(2,1)S(1)}, bf16[16,3,256,128]{3,2,1,0:T(8,128)(2,1)}, u32[]{:S(2)}) %copy-start) | copy-done | bytes 3145752
  61.8 20.6 %shard_map.83 = (f32[72,256,128]{2,1,0:T(8,128)}, f32[256,128]{1,0:T(8,128)S(1)}) custom-call(s32[72]{0:T(128)S(1)} %get-tuple-element.31.slot_ref, s32[72]{0:T(128)S(1)} %get-tuple-element.30.row_ref, s32[72]{0:T(128)S(1)} %get-tuple-element.29.vis_ref, bf16[72,128,1024]{2,1,0:T(8,128)(2,1)} %get-tuple-element.16.refs_0_.refs_1_.refs_2_.refs_3_, ...), custom_call_target="tpu_custom_call" | custom-call | tf_op jit(solution)/shard_map/pallas_call | solution.py:554
  82.6 0.2 dynamic_update_slice.3.m_ref
  82.8 0.6 copy-done.2
  83.4 15.4 %shard_map.84 = f32[48,256]{1,0:T(8,128)} custom-call(f32[48,256]{1,0:T(8,128)} %copy-done.2), custom_call_target="tpu_custom_call" | custom-call | tf_op jit(solution)/shard_map/pallas_call | solution.py:413
  98.9 0.7 constant_dynamic-slice_fusion
  99.7 0.9 copy.32
  100.7 18.4 %shard_map.85 = (bf16[48,256,128]{2,1,0:T(8,128)(2,1)S(1)}, f32[256,128]{1,0:T(8,128)S(1)}) custom-call(s32[72]{0:T(128)S(1)} %get-tuple-element.31.slot_ref, s32[72]{0:T(128)S(1)} %get-tuple-element.30.row_ref, s32[72]{0:T(128)S(1)} %get-tuple-element.29.vis_ref, bf16[72,128,1024]{2,1,0:T(8,128)(2,1)} %get-tuple-element.15.refs_0_.refs_1_.refs_2_.refs_3_, ...), custom_call_target="tpu_custom_call" | custom-call | tf_op jit(solution)/shard_map/pallas_call | solution.py:588
  119.2 26.8 %shard_map.86 = (f32[768,128]{1,0:T(8,128)S(1)}, f32[3,256]{1,0:T(4,128)S(1)}) custom-call(bf16[16,768,128]{2,1,0:T(8,128)(2,1)S(1)} %bitcast.56, f32[16,3,256]{2,1,0:T(4,128)S(1)} %reshape.155.l_ref), custom_call_target="tpu_custom_call" | custom-call | tf_op jit(solution)/shard_map/pallas_call | solution.py:510
  146.1 0.7 copy-done.1
  146.9 1.5 %fusion.2 = bf16[3,4,8,8,128]{4,3,1,2,0:T(8,128)(2,1)S(1)} fusion(f32[3,8,32,128]{3,2,1,0:T(8,128)} %bitcast.57, bf16[2,256,1024]{2,1,0:T(8,128)(2,1)} %get-tuple-element.20, f32[3,8,32]{2,1,0:T(8,128)S(1)} %add.76, f32[3,8,32,4]{2,3,1,0:T(4,128)S(1)} %get-tuple-element.33, f32[3,8,32]{2,1,0:T(8,128)S(1)} %sub.49, bf16[3,4,512]{2,1,0:T(4,128)(2,1)S(1)} %copy-done.3), kind=kOutput, calls=%fused_computation.3 | convolution fusion | flops 7391232 | bytes 1193984 | tf_op jit(solution)/shard_map/bgrt,btgd->bgrd/dot_general | solution.py:613
  148.5 0.7 reshape.160
  (24 shorter events, 0.6 us)
Async XLA Ops:
  0.0 58.4 %copy-start.3 = (bf16[3,4,512]{2,1,0:T(4,128)(2,1)S(1)}, bf16[3,4,512]{2,1,0:T(4,128)(2,1)}, u32[]{:S(2)}) copy-start(bf16[3,4,512]{2,1,0:T(4,128)(2,1)} %param.10) | copy-start | bytes 36868
  60.0 1.9 %copy-start = (bf16[16,3,256,128]{3,2,1,0:T(8,128)(2,1)S(1)}, bf16[16,3,256,128]{3,2,1,0:T(8,128)(2,1)}, u32[]{:S(2)}) copy-start(bf16[16,3,256,128]{3,2,1,0:T(8,128)(2,1)} %get-tuple-element.17) | copy-start | bytes 9437188
  82.8 0.6 copy-start.2
  146.1 0.7 copy-start.1
